TPU v7x, 32 devices: a whole 2x2x4 slice. The times are simulated.
32 devices in a mesh: nodes: 8 (over y, x, core), queries: 4 (over z).
Axes of the slice: x: 2, y: 2, z: 4, core: 2. Of those that a mesh axis runs over, the one named last changes fastest.
Arguments:
- state_in: float32 [2048, 512], P('nodes', 'queries')
- edge_src: int32 [32768], P('nodes'), may hold values from 0 to 767
- edge_dst: int32 [32768], P('nodes'), may hold values from 0 to 255
- edge_rel: int32 [32768], P('nodes'), may hold values from 0 to 534
- edge_count: int32 [8], P('nodes'), may hold values from 1024 to 4096, as said below
- send_list: int32 [8, 8, 64], P('nodes'), may hold values from 0 to 255
- query_head: int32 [16], P('queries'), may hold values from 0 to 2047
- query_rel: int32 [16], P('queries'), may hold values from 0 to 534
- pos_tail: int32 [16], P('queries'), may hold values from 0 to 2047
- neg_ids: int32 [16, 1024], P('queries', 'nodes'), may hold values from 0 to 255
- rel_table: float32 [535, 32], replicated, may hold values from -1.8 to 1.8
- layer_weight: float32 [32, 32], replicated, may hold values from -1 to 1
- mlp_entity: float32 [32, 64], replicated, may hold values from -1 to 1
- mlp_query: float32 [32, 64], replicated, may hold values from -1 to 1
- score_weight: float32 [64], replicated, may hold values from -0.75 to 0.75
Outputs:
- new_state: float32 [2048, 512], P('nodes', 'queries')
- loss: float32 [16], P('queries')
- grad_rel: float32 [535, 32], replicated
- grad_layer: float32 [32, 32], replicated
- grad_entity: float32 [32, 64], replicated
- grad_query: float32 [32, 64], replicated
- grad_score: float32 [64], replicated
Inputs may be any that keep to these rules, and one draw needn't show every extreme that they name: `edge_count`: some partition holds exactly 4096 live edges.
All inputs are finite; a program needn't handle non-finite values.
Results may differ from a plain program's by a relative error of at most 0.0003.
Values sent between devices are 32-bit elements; how exact they have to be, the bound alone decides.
No kernel may reach another device: no remote copies, remote signals or barrier semaphores. Data moves between devices by JAX's collectives and lax.ppermute only.
A program may use at most 64 MiB of HBM per device.

v0:
```python
import functools

import jax
import jax.numpy as jnp
from jax import lax
from jax.experimental import pallas as pl
from jax.experimental.pallas import tpu as pltpu
from jax.sharding import PartitionSpec as P

adversarial = 0.5
HIGH = lax.Precision.HIGHEST
F32 = jnp.float32
BF16 = jnp.bfloat16
LANES = 128
SUBLANES = 8
FORWARD = 3
BACKWARD = 2


def pad_to(count, unit):
    return -(-count // unit) * unit


def split(values, pieces, axis=0):
    found = []
    for _ in range(pieces):
        piece = values.astype(BF16)
        values = values - piece.astype(F32)
        found.append(piece)
    return jnp.concatenate(found, axis=axis)


def join(values, pieces, axis=0):
    size = values.shape[axis] // pieces
    parts = [
        lax.slice_in_dim(values, piece * size, (piece + 1) * size, axis=axis)
        for piece in range(pieces)
    ]
    return functools.reduce(jnp.add, parts)


def one_hot(index_row, rows):
    spots = lax.broadcasted_iota(jnp.int32, (rows, index_row.shape[1]), 0)
    return (spots == index_row).astype(F32).astype(BF16)


def dot_nn(left, right, precision=None):
    return lax.dot_general(
        left, right, (((1,), (0,)), ((), ())), precision=precision, preferred_element_type=F32
    )


def dot_nt(left, right, precision=None):
    return lax.dot_general(
        left, right, (((1,), (1,)), ((), ())), precision=precision, preferred_element_type=F32
    )


def local_row(entity, ent_local):
    node = lax.axis_index("nodes")
    return jnp.where(entity // ent_local == node, entity % ent_local, -1)


def in_lanes(small_row):
    lane = lax.broadcasted_iota(jnp.int32, (1, LANES), 1)
    found = jnp.full((1, LANES), -1, jnp.int32)
    for spot in range(small_row.shape[1]):
        found = jnp.where(lane == spot, small_row[:, spot : spot + 1], found)
    return found


def as_column(row):
    size = row.shape[1]
    across = lax.broadcasted_iota(jnp.int32, (size, size), 1)
    down = lax.broadcasted_iota(jnp.int32, (size, size), 0)
    return jnp.sum(jnp.where(across == down, row, 0.0), axis=1, keepdims=True)


def on_diagonal(block, times):
    size = block.shape[0]
    wide = jnp.concatenate([jnp.concatenate([block] * times, axis=1)] * times, axis=0)
    across = lax.broadcasted_iota(jnp.int32, wide.shape, 1) // size
    down = lax.broadcasted_iota(jnp.int32, wide.shape, 0) // size
    return jnp.where(across == down, wide, 0.0)


def send_kernel(send_ref, state_ref, out_ref):
    count, bound = send_ref.shape
    ent = state_ref.shape[0]
    pieces = split(state_ref[...], FORWARD, axis=1)
    wanted = send_ref[...].T
    entity = lax.broadcasted_iota(jnp.int32, (bound, ent), 1)
    for n in range(count):
        hot = (entity == wanted[:, n : n + 1]).astype(F32).astype(BF16)
        out_ref[n] = join(dot_nn(hot, pieces), FORWARD, axis=1)


def early_kernel(sizes, state_ref, src_ref, rel_ref, table_ref, local_ref, relation_ref):
    chunk, = sizes
    ent = state_ref.shape[0]
    width, relations = table_ref.shape
    edges = src_ref.shape[1]
    rel_rows = pad_to(relations, 16)
    state_bits = split(state_ref[...].T, FORWARD)
    rel_bits = split(table_ref[...], FORWARD)
    rel_bits = jnp.concatenate(
        [rel_bits, jnp.zeros((FORWARD * width, rel_rows - relations), BF16)], axis=1
    )
    for start in range(0, edges, chunk):
        span = slice(start, start + chunk)
        local_ref[:, span] = join(dot_nn(state_bits, one_hot(src_ref[:, span], ent)), FORWARD)
        relation_ref[:, span] = join(
            dot_nn(rel_bits, one_hot(rel_ref[:, span], rel_rows)), FORWARD
        )


def forward_kernel(
    sizes,
    count_ref,
    head_ref,
    qrel_ref,
    tail_ref,
    state_ref,
    recv_ref,
    src_ref,
    dst_ref,
    neg_ref,
    local_ref,
    relation_ref,
    table_ref,
    layer_ref,
    ment_ref,
    mquery_ref,
    score_ref,
    new_ref,
    srct_ref,
    entity_ref,
    columns_ref,
    totals_ref,
):
    chunk, queries_total = sizes
    ent = state_ref.shape[0]
    edges = src_ref.shape[1]
    width, relations = table_ref.shape
    hid = ment_ref.shape[1]
    q_local, neg = neg_ref.shape
    blocks = q_local * width
    recv_bits = split(recv_ref[...].T, FORWARD)
    live = count_ref[...]
    total = jnp.zeros((FORWARD * blocks, ent), F32)
    for start in range(0, edges, chunk):
        span = slice(start, start + chunk)
        far = one_hot(src_ref[:, span] - ent, recv_bits.shape[1])
        source = local_ref[:, span] + join(dot_nn(recv_bits, far), FORWARD)
        srct_ref[:, span] = source
        message = source * jnp.concatenate([relation_ref[:, span]] * q_local, axis=0)
        spot = lax.broadcasted_iota(jnp.int32, (1, chunk), 1) + start
        ends = jnp.where(spot < live, dst_ref[:, span], -1)
        total = total + dot_nt(split(message, FORWARD), one_hot(ends, ent))
    summed = join(total, FORWARD)

    entity_row = lax.broadcasted_iota(jnp.int32, (1, ent), 1)
    lane_row = lax.broadcasted_iota(jnp.int32, (1, LANES), 1)
    heads = local_row(head_ref[...], ent)
    tails = in_lanes(local_row(tail_ref[...], ent))
    table_bits = jnp.concatenate(
        [
            split(table_ref[...], FORWARD),
            jnp.zeros((FORWARD * width, pad_to(relations, LANES) - relations), BF16),
        ],
        axis=1,
    )
    qvec = join(dot_nn(table_bits, one_hot(in_lanes(qrel_ref[...]), table_bits.shape[1])), FORWARD)
    seeds = [
        qvec[:, q : q + 1] * (entity_row == heads[:, q : q + 1]).astype(F32)
        for q in range(q_local)
    ]
    summed = summed + jnp.concatenate(seeds, axis=0)
    pre = dot_nn(on_diagonal(layer_ref[...].T, q_local), summed, HIGH)
    entity_ref[:blocks, :] = summed
    entity_ref[blocks:, :] = pre
    new_t = state_ref[...].T + jnp.maximum(pre, 0.0)
    new_ref[...] = new_t.T

    for q in range(q_local):
        own = new_t[q * width : (q + 1) * width]
        hot = one_hot(neg_ref[q : q + 1, :], ent)
        columns_ref[:width, q * neg : (q + 1) * neg] = join(
            dot_nn(split(own, FORWARD), hot), FORWARD
        )
    every = join(dot_nn(split(new_t, FORWARD), one_hot(tails, ent)), FORWARD)
    positive = jnp.zeros((width, LANES), F32)
    for q in range(q_local):
        positive = positive + jnp.where(lane_row == q, every[q * width : (q + 1) * width], 0.0)
    last = slice(q_local * neg, q_local * neg + LANES)
    columns_ref[:width, last] = positive
    count = q_local * neg + LANES
    query_part = dot_nn(mquery_ref[...].T, qvec, HIGH)
    plain = dot_nn(ment_ref[...].T, columns_ref[:width, :count], HIGH)
    for q in range(q_local):
        span = slice(q * neg, (q + 1) * neg)
        columns_ref[width : width + hid, span] = plain[:, span] + query_part[:, q : q + 1]
    columns_ref[width : width + hid, last] = plain[:, last] + query_part
    columns_ref[:width, count:] = qvec
    columns_ref[width : width + hid, count:] = jnp.zeros((hid, LANES), F32)
    hidden = columns_ref[width : width + hid, :count]
    scores = jnp.sum(
        jnp.maximum(hidden, 0.0) * as_column(score_ref[...]), axis=0, keepdims=True
    )
    part_total = jnp.zeros((1, LANES), F32)
    part_weighted = jnp.zeros((1, LANES), F32)
    base = width + hid
    columns_ref[base:, :] = jnp.zeros((SUBLANES, count + LANES), F32)
    for q in range(q_local):
        span = slice(q * neg, (q + 1) * neg)
        mine = scores[:, span]
        weights = jnp.exp(adversarial * mine)
        decay = jnp.exp(-jnp.abs(mine))
        softplus = jnp.maximum(mine, 0.0) + jnp.log1p(decay)
        own = jnp.sum(weights, axis=1, keepdims=True)
        part_total = jnp.where(lane_row == q, own, part_total)
        part_weighted = jnp.where(
            lane_row == q, jnp.sum(weights * softplus, axis=1, keepdims=True), part_weighted
        )
        sigmoid = jnp.where(mine >= 0.0, 1.0, decay) / (1.0 + decay)
        share = weights / jnp.where(own > 0.0, own, 1.0)
        columns_ref[base : base + 1, span] = share * sigmoid * (1.0 / queries_total)
        columns_ref[base + 1 : base + 2, span] = neg_ref[q : q + 1, :].astype(F32)
    final = scores[:, last]
    decay = jnp.exp(-jnp.abs(final))
    present = tails >= 0
    part_positive = jnp.where(present, jnp.maximum(-final, 0.0) + jnp.log1p(decay), 0.0)
    missing = jnp.where(final >= 0.0, decay, 1.0) / (1.0 + decay)
    columns_ref[base : base + 1, last] = jnp.where(present, -missing, 0.0) * (1.0 / queries_total)
    columns_ref[base + 1 : base + 2, last] = tails.astype(F32)
    columns_ref[base : base + 1, count:] = in_lanes(heads).astype(F32)
    columns_ref[base + 1 : base + 2, count:] = in_lanes(qrel_ref[...]).astype(F32)
    tile = jnp.concatenate(
        [part_total, part_weighted, part_positive, jnp.zeros((5, LANES), F32)], axis=0
    )
    for n in range(totals_ref.shape[0]):
        totals_ref[n] = tile


def backward_kernel(
    sizes,
    count_ref,
    srct_ref,
    dst_ref,
    rel_ref,
    layer_ref,
    ment_ref,
    mquery_ref,
    score_ref,
    entity_ref,
    columns_ref,
    out_ref,
):
    chunk, relations, q_local, neg = sizes
    width, hid = ment_ref.shape
    ent = entity_ref.shape[1]
    edges = dst_ref.shape[1]
    blocks = q_local * width
    count = q_local * neg + LANES
    last = slice(q_local * neg, count)
    base = width + hid
    rel_lanes = pad_to(relations, LANES)
    rel_rows = pad_to(relations, 16)
    picked = columns_ref[:width, :count]
    hidden = columns_ref[width:base, :count]
    qvec = columns_ref[:width, count:]
    coef = columns_ref[base : base + 1, :count]
    picks = columns_ref[base + 1 : base + 2, :count].astype(jnp.int32)
    heads = columns_ref[base : base + 1, count:].astype(jnp.int32)
    qrels = columns_ref[base + 1 : base + 2, count:].astype(jnp.int32)
    tails = picks[:, last]
    grad_hidden = jnp.where(hidden > 0.0, coef * as_column(score_ref[...]), 0.0)
    active = jnp.maximum(hidden, 0.0)
    both = jnp.concatenate([ment_ref[...], mquery_ref[...]], axis=0)
    grad_both = dot_nn(both, grad_hidden, HIGH)
    entity_row = lax.broadcasted_iota(jnp.int32, (1, ent), 1)
    rel_row = lax.broadcasted_iota(jnp.int32, (1, rel_lanes), 1)
    layer = on_diagonal(layer_ref[...], q_local)
    summed = entity_ref[:blocks, :]
    gate = entity_ref[blocks:, :] > 0.0

    cubes, tail_cubes = [], []
    for q in range(q_local):
        span = slice(q * neg, (q + 1) * neg)
        hot = one_hot(picks[:, span], ent)
        cubes.append(join(dot_nt(split(grad_both[:width, span], BACKWARD), hot), BACKWARD))
        spot = q_local * neg + q
        at_tail = (entity_row == tails[:, q : q + 1]).astype(F32)
        tail_cubes.append(grad_both[:width, spot : spot + 1] * at_tail)
    grad_pre = jnp.where(gate, jnp.concatenate(cubes, axis=0), 0.0)
    tail_pre = jnp.where(gate, jnp.concatenate(tail_cubes, axis=0), 0.0)
    grad_sum = dot_nn(layer, grad_pre, HIGH)
    tail_sum = dot_nn(layer, tail_pre, HIGH)
    grad_layer = dot_nt(summed, grad_pre, HIGH)
    tail_layer = dot_nt(summed, tail_pre, HIGH)

    seeds = []
    tail_seed = jnp.zeros((width, rel_lanes), F32)
    layer_parts = []
    tail_part = jnp.zeros((width, width), F32)
    for q in range(q_local):
        rows = slice(q * width, (q + 1) * width)
        span = slice(q * neg, (q + 1) * neg)
        spot = q_local * neg + q
        at_head = (entity_row == heads[:, q : q + 1]).astype(F32)
        at_rel = (rel_row == qrels[:, q : q + 1]).astype(F32)
        grad_qvec = jnp.sum(grad_both[width:, span], axis=1, keepdims=True) + jnp.sum(
            grad_sum[rows] * at_head, axis=1, keepdims=True
        )
        seeds.append(grad_qvec * at_rel)
        tail_qvec = grad_both[width:, spot : spot + 1] + jnp.sum(
            tail_sum[rows] * at_head, axis=1, keepdims=True
        )
        tail_seed = tail_seed + tail_qvec * at_rel
        layer_parts.append(grad_layer[rows, rows])
        tail_part = tail_part + tail_layer[rows, rows]
    seeds.append(tail_seed)
    layer_parts.append(tail_part)
    spare = out_ref.shape[1] - rel_lanes - width - 3 * hid
    for block in range(q_local + 1):
        if block < q_local:
            span = slice(block * neg, (block + 1) * neg)
            vectors = jnp.broadcast_to(qvec[:, block : block + 1], (width, neg))
        else:
            span, vectors = last, qvec
        size = span.stop - span.start
        entity_part = dot_nt(picked[:, span], grad_hidden[:, span], HIGH)
        query_part = dot_nt(vectors, grad_hidden[:, span], HIGH)
        score_part = dot_nt(
            jnp.broadcast_to(coef[:, span], (width, size)), active[:, span], HIGH
        )
        rest = [layer_parts[block], entity_part, query_part, score_part]
        rest.append(jnp.zeros((width, spare), F32))
        out_ref[block * width : (block + 1) * width, rel_lanes:] = jnp.concatenate(rest, axis=1)

    sum_bits = split(grad_sum, BACKWARD)
    tail_column = jnp.sum(tail_sum, axis=1, keepdims=True)
    live = count_ref[...]
    total = jnp.zeros((BACKWARD * (blocks + width), rel_rows), F32)
    for start in range(0, edges, chunk):
        span = slice(start, start + chunk)
        spot = lax.broadcasted_iota(jnp.int32, (1, chunk), 1) + start
        ends = jnp.where(spot < live, dst_ref[:, span], -2)
        source = srct_ref[:, span]
        upstream = join(dot_nn(sum_bits, one_hot(ends, ent)), BACKWARD)
        tail_terms = jnp.zeros((width, chunk), F32)
        for q in range(q_local):
            rows = slice(q * width, (q + 1) * width)
            hit = (ends == tails[:, q : q + 1]).astype(F32)
            tail_terms = tail_terms + (tail_column[rows] * hit) * source[rows]
        terms = jnp.concatenate([upstream * source, tail_terms], axis=0)
        total = total + dot_nt(split(terms, BACKWARD), one_hot(rel_ref[:, span], rel_rows))
    gathered = join(total, BACKWARD)
    if rel_lanes > rel_rows:
        gathered = jnp.concatenate(
            [gathered, jnp.zeros((blocks + width, rel_lanes - rel_rows), F32)], axis=1
        )
    out_ref[:, :rel_lanes] = gathered + jnp.concatenate(seeds, axis=0)


def combine_kernel(sizes, totals_ref, own_ref, grads_ref, sent_ref, loss_ref):
    q_local, width = sizes
    everyone = jnp.sum(totals_ref[...], axis=0)
    total = everyone[0:1, :]
    scale = own_ref[0, 0:1, :] / total
    loss_ref[...] = (everyone[2:3, :] + everyone[1:2, :] / total)[:, :q_local]
    mixed = grads_ref[q_local * width :, :]
    for q in range(q_local):
        mixed = mixed + grads_ref[q * width : (q + 1) * width, :] * scale[:, q : q + 1]
    across = mixed.shape[1] // LANES
    tiles = width // SUBLANES * across
    for tile in range(tiles):
        top, left = tile // across * SUBLANES, tile % across * LANES
        sent_ref[tile] = mixed[top : top + SUBLANES, left : left + LANES]
    for tile in range(tiles, sent_ref.shape[0]):
        sent_ref[tile] = jnp.zeros((SUBLANES, LANES), F32)


def spread_kernel(parts_ref, out_ref):
    total = jnp.sum(parts_ref[...], axis=0)
    for n in range(out_ref.shape[0]):
        out_ref[n] = total


def unpack_kernel(sizes, tiles_ref, rel_ref, layer_ref, ment_ref, mquery_ref, score_ref):
    relations, across = sizes
    width, hid = ment_ref.shape
    down = width // SUBLANES
    flat = jnp.concatenate(
        [
            jnp.concatenate([tiles_ref[row * across + tile] for tile in range(across)], axis=1)
            for row in range(down)
        ],
        axis=0,
    )
    rel_lanes = pad_to(relations, LANES)
    rel_ref[...] = flat[:, :relations]
    start = rel_lanes
    layer_ref[...] = flat[:, start : start + width]
    start += width
    ment_ref[...] = flat[:, start : start + hid]
    start += hid
    mquery_ref[...] = flat[:, start : start + hid]
    start += hid
    score_ref[...] = flat[0:1, start : start + hid]


def vmem(count):
    return [pl.BlockSpec(memory_space=pltpu.VMEM)] * count


def call(kernel, name, outs, flops, *operands):
    found = pl.pallas_call(
        kernel,
        out_shape=tuple(jax.ShapeDtypeStruct(dims, F32) for dims in outs),
        in_specs=vmem(len(operands)),
        out_specs=tuple(vmem(len(outs))),
        compiler_params=pltpu.CompilerParams(vmem_limit_bytes=40 * 1024 * 1024),
        cost_estimate=pl.CostEstimate(flops=flops, bytes_accessed=1 << 20, transcendentals=0),
        name=name,
    )(*operands)
    return found[0] if len(outs) == 1 else found


def swap(values, axes):
    return lax.all_to_all(values, axes, split_axis=0, concat_axis=0, tiled=True)


def body(
    state_in,
    edge_src,
    edge_dst,
    edge_rel,
    edge_count,
    send_list,
    query_head,
    query_rel,
    pos_tail,
    neg_ids,
    rel_table,
    layer_weight,
    mlp_entity,
    mlp_query,
    score_weight,
):
    nodes = lax.axis_size("nodes")
    queries = lax.axis_size("queries")
    ent, width_all = state_in.shape
    relations, width = rel_table.shape
    hid = mlp_entity.shape[1]
    q_local = width_all // width
    edges = edge_src.shape[0]
    bound = send_list.shape[2]
    neg = neg_ids.shape[1]
    columns = q_local * neg + 2 * LANES
    chunk = min(512, edges)
    src_row = edge_src.reshape(1, edges)
    dst_row = edge_dst.reshape(1, edges)
    rel_row = edge_rel.reshape(1, edges)
    count = edge_count.reshape(1, 1)
    score_row = score_weight.reshape(1, hid)
    table_t = rel_table.T
    outgoing = call(
        send_kernel, "send", [(nodes, bound, width_all)], 10**9, send_list[0], state_in
    )
    received = swap(outgoing, "nodes").reshape(nodes * bound, width_all)
    local, relation = call(
        functools.partial(early_kernel, (chunk,)),
        "early",
        [(width_all, edges), (width, edges)],
        4 * 10**9,
        state_in,
        src_row,
        rel_row,
        table_t,
    )
    new_state, source_t, entity, cols, totals = call(
        functools.partial(forward_kernel, (chunk, q_local * queries)),
        "forward",
        [
            (ent, width_all),
            (width_all, edges),
            (2 * width_all, ent),
            (width + hid + SUBLANES, columns),
            (nodes, SUBLANES, LANES),
        ],
        4 * 10**9,
        count,
        query_head.reshape(1, q_local),
        query_rel.reshape(1, q_local),
        pos_tail.reshape(1, q_local),
        state_in,
        received,
        src_row,
        dst_row,
        neg_ids,
        local,
        relation,
        table_t,
        layer_weight,
        mlp_entity,
        mlp_query,
        score_row,
    )
    all_totals = swap(totals, "nodes")
    rel_lanes = pad_to(relations, LANES)
    lanes = rel_lanes + pad_to(width + 3 * hid, LANES)
    across = lanes // LANES
    grads = call(
        functools.partial(backward_kernel, (chunk, relations, q_local, neg)),
        "backward",
        [((q_local + 1) * width, lanes)],
        4 * 10**9,
        count,
        source_t,
        dst_row,
        rel_row,
        layer_weight,
        mlp_entity,
        mlp_query,
        score_row,
        entity,
        cols,
    )
    tiles = width // SUBLANES * across
    wide = nodes * queries
    group = wide if wide <= pad_to(tiles, nodes) else nodes
    held = pad_to(tiles, group)
    sent, loss = call(
        functools.partial(combine_kernel, (q_local, width)),
        "combine",
        [(held, SUBLANES, LANES), (1, q_local)],
        10**6,
        all_totals,
        totals,
        grads,
    )
    axes = ("nodes", "queries") if group == wide else "nodes"
    own = held // group
    parts = swap(sent, axes).reshape(group, own * SUBLANES, LANES)
    if group == wide:
        mine = call(spread_kernel, "spread", [(group, own * SUBLANES, LANES)], 10**6, parts)
    else:
        mine = lax.psum(jnp.sum(parts, axis=0), "queries")
        mine = jnp.broadcast_to(mine, (group,) + mine.shape)
    final = swap(mine, axes).reshape(held, SUBLANES, LANES)
    grad_rel, grad_layer, grad_entity, grad_query, grad_score = call(
        functools.partial(unpack_kernel, (relations, across)),
        "unpack",
        [(width, relations), (width, width), (width, hid), (width, hid), (1, hid)],
        10**6,
        final,
    )
    return (
        new_state,
        loss.reshape(q_local),
        grad_rel.T,
        grad_layer,
        grad_entity,
        grad_query,
        grad_score.reshape(hid),
    )


def solution(mesh):
    in_specs = (
        P("nodes", "queries"),
        P("nodes"),
        P("nodes"),
        P("nodes"),
        P("nodes"),
        P("nodes", None, None),
        P("queries"),
        P("queries"),
        P("queries"),
        P("queries", "nodes"),
        P(),
        P(),
        P(),
        P(),
        P(),
    )
    out_specs = (P("nodes", "queries"), P("queries"), P(), P(), P(), P(), P())
    return jax.shard_map(body, mesh=mesh, in_specs=in_specs, out_specs=out_specs, check_vma=False)
```

profile of v0, /device:TPU:0, one launch (start us, length us, event | category | flops | bytes accessed | tf_op | source)
XLA Modules:
  0.0 60.0 jit_solution(5156201925119247346)
XLA Ops:
  0.6 0.9 %copy-done = f32[256,128]{1,0:T(8,128)S(1)} copy-done((f32[256,128]{1,0:T(8,128)S(1)}, f32[256,128]{1,0:T(8,128)}, u32[]{:S(2)}) %copy-start) | copy-done | bytes 131096
  1.5 0.7 %copy-done.9 = s32[1,8,64]{2,1,0:T(8,128)S(1)} copy-done((s32[1,8,64]{2,1,0:T(8,128)S(1)}, s32[1,8,64]{2,1,0:T(8,128)}, u32[]{:S(2)}) %copy-start.9) | copy-done | bytes 2072
  2.2 1.2 %send.1 = f32[8,64,128]{2,1,0:T(8,128)} custom-call(s32[8,64]{1,0:T(8,128)S(1)} %bitcast.25, f32[256,128]{1,0:T(8,128)S(1)} %copy-done), custom_call_target="tpu_custom_call" | custom-call | flops 1000000000 | bytes 1048576 | tf_op jit(solution)/shard_map/send/pallas_call | solution.py:418
  3.4 5.2 %all-to-all-start = ((f32[8,64,128]{2,1,0:T(8,128)}), f32[8,64,128]{2,1,0:T(8,128)S(1)}, u32[]{:S(2)}, u32[]{:S(2)}) async-start(f32[8,64,128]{2,1,0:T(8,128)} %send.1), calls=%async_computation | async-start | bytes 524288 | tf_op jit(solution)/shard_map/all_to_all | solution.py:431
  9.3 0.0 copy-start.6
  9.3 0.0 copy-start.7
  9.3 0.0 copy-start.11
  9.4 0.0 copy-start.12
  9.4 0.0 copy-start.14
  9.4 1.9 %early.1 = (f32[128,4096]{1,0:T(8,128)S(1)}, f32[32,4096]{1,0:T(8,128)S(1)}) custom-call(f32[256,128]{1,0:T(8,128)S(1)} %copy-done.1, s32[1,4096]{1,0:T(1,128)S(1)} %bitcast.19, s32[1,4096]{1,0:T(1,128)S(1)} %bitcast.23, f32[32,535]{1,0:T(8,128)S(1)} %bitcast.17), custom_call_target="tpu_custom_call" | custom-call | flops 4000000000 | bytes 1048576 | tf_op jit(solution)/shard_map/early/pallas_call | solution.py:418
  11.3 1.3 %copy-done.15 = f32[128,4096]{1,0:T(8,128)} copy-done((f32[128,4096]{1,0:T(8,128)}, f32[128,4096]{1,0:T(8,128)S(1)}, u32[]{:S(2)}) %copy-start.15) | copy-done | bytes 2097176
  12.7 2.9 %all-to-all-done = f32[8,64,128]{2,1,0:T(8,128)S(1)} async-done(((f32[8,64,128]{2,1,0:T(8,128)}), f32[8,64,128]{2,1,0:T(8,128)S(1)}, u32[]{:S(2)}, u32[]{:S(2)}) %all-to-all-start) | async-done | bytes 262176 | tf_op jit(solution)/shard_map/all_to_all | solution.py:431
  15.6 1.6 %copy-done.16 = f32[128,4096]{1,0:T(8,128)S(1)} copy-done((f32[128,4096]{1,0:T(8,128)S(1)}, f32[128,4096]{1,0:T(8,128)}, u32[]{:S(2)}) %copy-start.16) | copy-done | bytes 2097176
  17.2 4.6 %forward.1 = (f32[256,128]{1,0:T(8,128)}, f32[128,4096]{1,0:T(8,128)S(1)}, f32[256,256]{1,0:T(8,128)S(1)}, f32[104,768]{1,0:T(8,128)S(1)}, f32[8,8,128]{2,1,0:T(8,128)}) custom-call(s32[1,1]{1,0:T(1,128)} %bitcast.14.count_ref, s32[1,4]{1,0:T(1,128)S(1)} %bitcast.26, s32[1,4]{1,0:T(1,128)S(1)} %bitcast.27, s32[1,4]{1,0:T(1,128)S(1)} %bitcast.28, ...), custom_call_target="tpu_custom_call" | custom-call | flops 4000000000 | bytes 1048576 | tf_op jit(solution)/shard_map/forward/pallas_call | solution.py:418
  21.8 0.7 %copy-done.17 = f32[104,768]{1,0:T(8,128)} copy-done((f32[104,768]{1,0:T(8,128)}, f32[104,768]{1,0:T(8,128)S(1)}, u32[]{:S(2)}) %copy-start.17) | copy-done | bytes 319512
  22.5 0.7 %copy-done.19 = f32[256,256]{1,0:T(8,128)} copy-done((f32[256,256]{1,0:T(8,128)}, f32[256,256]{1,0:T(8,128)S(1)}, u32[]{:S(2)}) %copy-start.19) | copy-done | bytes 262168
  23.2 3.3 %all-to-all-start.1 = ((f32[8,8,128]{2,1,0:T(8,128)}), f32[8,8,128]{2,1,0:T(8,128)S(1)}, u32[]{:S(2)}, u32[]{:S(2)}) async-start(f32[8,8,128]{2,1,0:T(8,128)} %get-tuple-element.24.own_ref), calls=%async_computation.1 | async-start | bytes 65536 | tf_op jit(solution)/shard_map/all_to_all | solution.py:431
  26.6 1.0 %copy-done.18 = f32[104,768]{1,0:T(8,128)S(1)} copy-done((f32[104,768]{1,0:T(8,128)S(1)}, f32[104,768]{1,0:T(8,128)}, u32[]{:S(2)}) %copy-start.18) | copy-done | bytes 319512
  27.5 0.9 %copy-done.20 = f32[256,256]{1,0:T(8,128)S(1)} copy-done((f32[256,256]{1,0:T(8,128)S(1)}, f32[256,256]{1,0:T(8,128)}, u32[]{:S(2)}) %copy-start.20) | copy-done | bytes 262168
  28.5 5.0 %backward.1.grads_ref = f32[160,896]{1,0:T(8,128)S(1)} custom-call(s32[1,1]{1,0:T(1,128)} %bitcast.15.count_ref, f32[128,4096]{1,0:T(8,128)S(1)} %get-tuple-element.25.srct_ref, s32[1,4096]{1,0:T(1,128)S(1)} %bitcast.22, s32[1,4096]{1,0:T(1,128)S(1)} %bitcast.24, f32[32,32]{1,0:T(8,128)S(1)} %copy-done.6, f32[32,64]{1,0:T(8,128)S(1)} %copy-done.7, ...), custom_call_target="tpu_custom_call" | custom-call | flops 4000000000 | bytes 1048576 | tf_op jit(solution)/shard_map/backward/pallas_call | solution.py:418
  33.5 1.3 %combine.1 = (f32[32,8,128]{2,1,0:T(8,128)S(1)}, f32[1,4]{1,0:T(1,128)}) custom-call(f32[8,8,128]{2,1,0:T(8,128)S(1)} %all-to-all-done.1.totals_ref, f32[8,8,128]{2,1,0:T(8,128)} %get-tuple-element.24.own_ref, f32[160,896]{1,0:T(8,128)S(1)} %backward.1.grads_ref), custom_call_target="tpu_custom_call" | custom-call | flops 1000000 | bytes 1048576 | tf_op jit(solution)/shard_map/combine/pallas_call | solution.py:418
  34.7 14.5 %all_to_all.20.parts_ref = f32[32,8,128]{2,1,0:T(8,128)S(1)} all-to-all(f32[32,8,128]{2,1,0:T(8,128)S(1)} %get-tuple-element.29), channel_id=1, replica_groups=mesh['nodes'=8,'queries'=4] {'nodes','queries'}, dimensions={0} | all-to-all | bytes 262144 | tf_op jit(solution)/shard_map/all_to_all | solution.py:431
  49.2 10.1 %all_to_all.21.tiles_ref = f32[32,8,128]{2,1,0:T(8,128)S(1)} all-to-all(f32[32,8,128]{2,1,0:T(8,128)S(1)} %spread.1), channel_id=1, replica_groups=mesh['nodes'=8,'queries'=4] {'nodes','queries'}, dimensions={0} | all-to-all | bytes 262144 | tf_op jit(solution)/shard_map/all_to_all | solution.py:431
  59.4 0.7 %unpack.1 = (f32[32,535]{1,0:T(8,128)}, f32[32,32]{1,0:T(8,128)}, f32[32,64]{1,0:T(8,128)}, f32[32,64]{1,0:T(8,128)}, f32[1,64]{1,0:T(1,128)}) custom-call(f32[32,8,128]{2,1,0:T(8,128)S(1)} %all_to_all.21.tiles_ref), custom_call_target="tpu_custom_call" | custom-call | flops 1000000 | bytes 1048576 | tf_op jit(solution)/shard_map/unpack/pallas_call | solution.py:418
  (31 shorter events, 0.1 us)
Async XLA Ops:
  0.6 0.9 %copy-start = (f32[256,128]{1,0:T(8,128)S(1)}, f32[256,128]{1,0:T(8,128)}, u32[]{:S(2)}) copy-start(f32[256,128]{1,0:T(8,128)} %state_ref.5) | copy-start | bytes 393220
  1.5 0.7 %copy-start.9 = (s32[1,8,64]{2,1,0:T(8,128)S(1)}, s32[1,8,64]{2,1,0:T(8,128)}, u32[]{:S(2)}) copy-start(s32[1,8,64]{2,1,0:T(8,128)} %param.20) | copy-start | bytes 6148
  2.2 7.0 %copy-start.1 = (f32[256,128]{1,0:T(8,128)S(1)}, f32[256,128]{1,0:T(8,128)}, u32[]{:S(2)}) copy-start(f32[256,128]{1,0:T(8,128)} %state_ref.5) | copy-start | bytes 393220
  2.2 7.0 %copy-start.2 = (f32[535,32]{0,1:T(8,128)S(1)}, f32[535,32]{0,1:T(8,128)}, u32[]{:S(2)}) copy-start(f32[535,32]{0,1:T(8,128)} %param.25) | copy-start | bytes 205444
  2.2 7.0 %copy-start.3 = (s32[4096]{0:T(1024)S(1)}, s32[4096]{0:T(1024)}, u32[]{:S(2)}) copy-start(s32[4096]{0:T(1024)} %param.16) | copy-start | bytes 49156
  2.2 7.0 %copy-start.5 = (s32[4096]{0:T(1024)S(1)}, s32[4096]{0:T(1024)}, u32[]{:S(2)}) copy-start(s32[4096]{0:T(1024)} %param.18) | copy-start | bytes 49156
  3.4 12.1 %all-to-all-start = ((f32[8,64,128]{2,1,0:T(8,128)}), f32[8,64,128]{2,1,0:T(8,128)S(1)}, u32[]{:S(2)}, u32[]{:S(2)}) async-start(f32[8,64,128]{2,1,0:T(8,128)} %send.1), calls=%async_computation | async-start | bytes 524288 | tf_op jit(solution)/shard_map/all_to_all | solution.py:431
  9.3 6.2 %copy-start.4 = (s32[4096]{0:T(1024)S(1)}, s32[4096]{0:T(1024)}, u32[]{:S(2)}) copy-start(s32[4096]{0:T(1024)} %param.17) | copy-start | bytes 49156
  9.3 6.2 %copy-start.6 = (f32[32,32]{1,0:T(8,128)S(1)}, f32[32,32]{1,0:T(8,128)}, u32[]{:S(2)}) copy-start(f32[32,32]{1,0:T(8,128)} %layer_ref.3) | copy-start | bytes 12292
  9.3 6.2 %copy-start.7 = (f32[32,64]{1,0:T(8,128)S(1)}, f32[32,64]{1,0:T(8,128)}, u32[]{:S(2)}) copy-start(f32[32,64]{1,0:T(8,128)} %ment_ref.3) | copy-start | bytes 24580
  9.3 6.2 %copy-start.8 = (f32[32,64]{1,0:T(8,128)S(1)}, f32[32,64]{1,0:T(8,128)}, u32[]{:S(2)}) copy-start(f32[32,64]{1,0:T(8,128)} %mquery_ref.3) | copy-start | bytes 24580
  9.3 6.2 %copy-start.10 = (s32[4,128]{1,0:T(4,128)S(1)}, s32[4,128]{1,0:T(4,128)}, u32[]{:S(2)}) copy-start(s32[4,128]{1,0:T(4,128)} %neg_ref.1) | copy-start | bytes 6148
  9.3 6.2 %copy-start.11 = (s32[4]{0:T(128)S(1)}, s32[4]{0:T(128)}, u32[]{:S(2)}) copy-start(s32[4]{0:T(128)} %param.21) | copy-start | bytes 52
  9.4 6.2 %copy-start.12 = (s32[4]{0:T(128)S(1)}, s32[4]{0:T(128)}, u32[]{:S(2)}) copy-start(s32[4]{0:T(128)} %param.22) | copy-start | bytes 52
  9.4 6.2 %copy-start.13 = (s32[4]{0:T(128)S(1)}, s32[4]{0:T(128)}, u32[]{:S(2)}) copy-start(s32[4]{0:T(128)} %param.23) | copy-start | bytes 52
  9.4 6.2 %copy-start.14 = (f32[64]{0:T(128)S(1)}, f32[64]{0:T(128)}, u32[]{:S(2)}) copy-start(f32[64]{0:T(128)} %param.29) | copy-start | bytes 772
  11.3 1.3 %copy-start.15 = (f32[128,4096]{1,0:T(8,128)}, f32[128,4096]{1,0:T(8,128)S(1)}, u32[]{:S(2)}) copy-start(f32[128,4096]{1,0:T(8,128)S(1)} %get-tuple-element.21.local_ref) | copy-start | bytes 6291460
  15.6 1.6 %copy-start.16 = (f32[128,4096]{1,0:T(8,128)S(1)}, f32[128,4096]{1,0:T(8,128)}, u32[]{:S(2)}) copy-start(f32[128,4096]{1,0:T(8,128)} %copy-done.15) | copy-start | bytes 6291460
  21.8 0.7 %copy-start.17 = (f32[104,768]{1,0:T(8,128)}, f32[104,768]{1,0:T(8,128)S(1)}, u32[]{:S(2)}) copy-start(f32[104,768]{1,0:T(8,128)S(1)} %get-tuple-element.27.columns_ref) | copy-start | bytes 958468
  22.5 0.7 %copy-start.19 = (f32[256,256]{1,0:T(8,128)}, f32[256,256]{1,0:T(8,128)S(1)}, u32[]{:S(2)}) copy-start(f32[256,256]{1,0:T(8,128)S(1)} %get-tuple-element.26.entity_ref) | copy-start | bytes 786436
  23.2 10.2 %all-to-all-start.1 = ((f32[8,8,128]{2,1,0:T(8,128)}), f32[8,8,128]{2,1,0:T(8,128)S(1)}, u32[]{:S(2)}, u32[]{:S(2)}) async-start(f32[8,8,128]{2,1,0:T(8,128)} %get-tuple-element.24.own_ref), calls=%async_computation.1 | async-start | bytes 65536 | tf_op jit(solution)/shard_map/all_to_all | solution.py:431
  26.6 1.0 %copy-start.18 = (f32[104,768]{1,0:T(8,128)S(1)}, f32[104,768]{1,0:T(8,128)}, u32[]{:S(2)}) copy-start(f32[104,768]{1,0:T(8,128)} %copy-done.17) | copy-start | bytes 958468
  27.5 0.9 %copy-start.20 = (f32[256,256]{1,0:T(8,128)S(1)}, f32[256,256]{1,0:T(8,128)}, u32[]{:S(2)}) copy-start(f32[256,256]{1,0:T(8,128)} %copy-done.19) | copy-start | bytes 786436
where the time goes:
time: 60.6 us; the launch traced here: 60 us
  blocking collectives  24.6 us (41%)
  Pallas kernels  14.7 us (24%)
  starting transfers between devices  8.51 us (14%)
  local copies, waits for them, and re-layouts  7.93 us (13%)
  waiting for transfers between devices  2.86 us (5%)
  between operations  1.5 us (2%)
    all_to_all x2, blocking collectives, swap(): return lax.all_to_all(values, axes, split_axis=0, concat_axis=0, tiled=True)  24.6 us
    pallas_call x7, Pallas kernels, call(): pl.pallas_call(kernel, out_shape=tuple((jax.ShapeDtypeStruct(dims, F32) f...  14.7 us
    all_to_all x2, starting transfers between devices, swap(): return lax.all_to_all(values, axes, split_axis=0, concat_axis=0, tiled=True)  8.51 us
    unnamed x42, local copies, waits for them, and re-layouts  7.93 us
    all_to_all x2, waiting for transfers between devices, swap(): return lax.all_to_all(values, axes, split_axis=0, concat_axis=0, tiled=True)  2.86 us
  transfers between devices with their start and end apart: 2, of which 1 were waited for; matrix products, arithmetic and copies ran while one was open for 0% of the time, Pallas kernels for 11%

commit v1 on v0

--- a/solution.py
+++ b/solution.py
@@ -15,6 +15,7 @@
 SUBLANES = 8
 FORWARD = 3
 BACKWARD = 2
+SEND_LIMIT = 64 << 20
 
 
 def pad_to(count, unit):
@@ -40,8 +41,15 @@
 
 
 def one_hot(index_row, rows):
-    spots = lax.broadcasted_iota(jnp.int32, (rows, index_row.shape[1]), 0)
-    return (spots == index_row).astype(F32).astype(BF16)
+    parts = []
+    for base in range(0, rows, 256):
+        size = min(256, rows - base)
+        local = index_row - base
+        key = jnp.where((local >= 0) & (local < size), local, -1).astype(F32).astype(BF16)
+        spots = lax.broadcasted_iota(jnp.int32, (size, index_row.shape[1]), 0)
+        same = spots.astype(F32).astype(BF16) == key
+        parts.append(jnp.where(same, jnp.ones((), BF16), jnp.zeros((), BF16)))
+    return parts[0] if len(parts) == 1 else jnp.concatenate(parts, axis=0)
 
 
 def dot_nn(left, right, precision=None):
@@ -84,7 +92,15 @@
     return jnp.where(across == down, wide, 0.0)
 
 
-def send_kernel(send_ref, state_ref, out_ref):
+def send_kernel(send_hbm, state_hbm, out_ref, send_ref, state_ref, sems):
+    copies = [
+        pltpu.make_async_copy(send_hbm, send_ref, sems.at[0]),
+        pltpu.make_async_copy(state_hbm, state_ref, sems.at[1]),
+    ]
+    for copy in copies:
+        copy.start()
+    for copy in copies:
+        copy.wait()
     count, bound = send_ref.shape
     ent = state_ref.shape[0]
     pieces = split(state_ref[...], FORWARD, axis=1)
@@ -134,7 +150,8 @@
     score_ref,
     new_ref,
     srct_ref,
-    entity_ref,
+    summed_ref,
+    gate_ref,
     columns_ref,
     totals_ref,
 ):
@@ -177,8 +194,8 @@
     ]
     summed = summed + jnp.concatenate(seeds, axis=0)
     pre = dot_nn(on_diagonal(layer_ref[...].T, q_local), summed, HIGH)
-    entity_ref[:blocks, :] = summed
-    entity_ref[blocks:, :] = pre
+    summed_ref[...] = summed
+    gate_ref[...] = (pre > 0.0).astype(F32).astype(BF16)
     new_t = state_ref[...].T + jnp.maximum(pre, 0.0)
     new_ref[...] = new_t.T
 
@@ -252,13 +269,14 @@
     ment_ref,
     mquery_ref,
     score_ref,
-    entity_ref,
+    summed_ref,
+    gate_ref,
     columns_ref,
     out_ref,
 ):
     chunk, relations, q_local, neg = sizes
     width, hid = ment_ref.shape
-    ent = entity_ref.shape[1]
+    ent = summed_ref.shape[1]
     edges = dst_ref.shape[1]
     blocks = q_local * width
     count = q_local * neg + LANES
@@ -281,8 +299,8 @@
     entity_row = lax.broadcasted_iota(jnp.int32, (1, ent), 1)
     rel_row = lax.broadcasted_iota(jnp.int32, (1, rel_lanes), 1)
     layer = on_diagonal(layer_ref[...], q_local)
-    summed = entity_ref[:blocks, :]
-    gate = entity_ref[blocks:, :] > 0.0
+    summed = summed_ref[...]
+    gate = gate_ref[...].astype(F32)
 
     cubes, tail_cubes = [], []
     for q in range(q_local):
@@ -292,8 +310,8 @@
         spot = q_local * neg + q
         at_tail = (entity_row == tails[:, q : q + 1]).astype(F32)
         tail_cubes.append(grad_both[:width, spot : spot + 1] * at_tail)
-    grad_pre = jnp.where(gate, jnp.concatenate(cubes, axis=0), 0.0)
-    tail_pre = jnp.where(gate, jnp.concatenate(tail_cubes, axis=0), 0.0)
+    grad_pre = gate * jnp.concatenate(cubes, axis=0)
+    tail_pre = gate * jnp.concatenate(tail_cubes, axis=0)
     grad_sum = dot_nn(layer, grad_pre, HIGH)
     tail_sum = dot_nn(layer, tail_pre, HIGH)
     grad_layer = dot_nt(summed, grad_pre, HIGH)
@@ -363,12 +381,10 @@
     out_ref[:, :rel_lanes] = gathered + jnp.concatenate(seeds, axis=0)
 
 
-def combine_kernel(sizes, totals_ref, own_ref, grads_ref, sent_ref, loss_ref):
+def combine_kernel(sizes, totals_ref, own_ref, grads_ref, sent_ref):
     q_local, width = sizes
-    everyone = jnp.sum(totals_ref[...], axis=0)
-    total = everyone[0:1, :]
+    total = jnp.sum(totals_ref[...], axis=0)[0:1, :]
     scale = own_ref[0, 0:1, :] / total
-    loss_ref[...] = (everyone[2:3, :] + everyone[1:2, :] / total)[:, :q_local]
     mixed = grads_ref[q_local * width :, :]
     for q in range(q_local):
         mixed = mixed + grads_ref[q * width : (q + 1) * width, :] * scale[:, q : q + 1]
@@ -387,7 +403,9 @@
         out_ref[n] = total
 
 
-def unpack_kernel(sizes, tiles_ref, rel_ref, layer_ref, ment_ref, mquery_ref, score_ref):
+def unpack_kernel(
+    sizes, tiles_ref, totals_ref, rel_ref, layer_ref, ment_ref, mquery_ref, score_ref, loss_ref
+):
     relations, across = sizes
     width, hid = ment_ref.shape
     down = width // SUBLANES
@@ -408,19 +426,28 @@
     mquery_ref[...] = flat[:, start : start + hid]
     start += hid
     score_ref[...] = flat[0:1, start : start + hid]
+    everyone = jnp.sum(totals_ref[...], axis=0)
+    loss = everyone[2:3, :] + everyone[1:2, :] / everyone[0:1, :]
+    loss_ref[...] = loss[:, : loss_ref.shape[1]]
 
 
 def vmem(count):
     return [pl.BlockSpec(memory_space=pltpu.VMEM)] * count
 
 
-def call(kernel, name, outs, flops, *operands):
+def call(kernel, name, outs, flops, *operands, scratch=(), limit=40 << 20, far=(), alias=None):
+    spaces = [pltpu.HBM if spot in far else pltpu.VMEM for spot in range(len(operands))]
     found = pl.pallas_call(
         kernel,
-        out_shape=tuple(jax.ShapeDtypeStruct(dims, F32) for dims in outs),
-        in_specs=vmem(len(operands)),
-        out_specs=tuple(vmem(len(outs))),
-        compiler_params=pltpu.CompilerParams(vmem_limit_bytes=40 * 1024 * 1024),
+        out_shape=tuple(
+            dims if isinstance(dims, jax.ShapeDtypeStruct) else jax.ShapeDtypeStruct(dims, F32)
+            for dims in outs
+        ),
+        in_specs=[pl.BlockSpec(memory_space=space) for space in spaces],
+        out_specs=tuple(pl.BlockSpec(memory_space=pltpu.VMEM) for _ in outs),
+        scratch_shapes=scratch,
+        input_output_aliases=alias or {},
+        compiler_params=pltpu.CompilerParams(vmem_limit_bytes=limit),
         cost_estimate=pl.CostEstimate(flops=flops, bytes_accessed=1 << 20, transcendentals=0),
         name=name,
     )(*operands)
@@ -466,7 +493,19 @@
     score_row = score_weight.reshape(1, hid)
     table_t = rel_table.T
     outgoing = call(
-        send_kernel, "send", [(nodes, bound, width_all)], 10**9, send_list[0], state_in
+        send_kernel,
+        "send",
+        [(nodes, bound, width_all)],
+        10**9,
+        send_list[0],
+        state_in,
+        scratch=[
+            pltpu.VMEM((nodes, bound), jnp.int32),
+            pltpu.VMEM((ent, width_all), F32),
+            pltpu.SemaphoreType.DMA((2,)),
+        ],
+        far=(0, 1),
+        limit=SEND_LIMIT,
     )
     received = swap(outgoing, "nodes").reshape(nodes * bound, width_all)
     local, relation = call(
@@ -479,13 +518,14 @@
         rel_row,
         table_t,
     )
-    new_state, source_t, entity, cols, totals = call(
+    new_state, source_t, summed, gate, cols, totals = call(
         functools.partial(forward_kernel, (chunk, q_local * queries)),
         "forward",
         [
             (ent, width_all),
             (width_all, edges),
-            (2 * width_all, ent),
+            (width_all, ent),
+            jax.ShapeDtypeStruct((width_all, ent), BF16),
             (width + hid + SUBLANES, columns),
             (nodes, SUBLANES, LANES),
         ],
@@ -506,6 +546,7 @@
         mlp_entity,
         mlp_query,
         score_row,
+        alias={9: 1},
     )
     all_totals = swap(totals, "nodes")
     rel_lanes = pad_to(relations, LANES)
@@ -524,17 +565,18 @@
         mlp_entity,
         mlp_query,
         score_row,
-        entity,
+        summed,
+        gate,
         cols,
     )
     tiles = width // SUBLANES * across
     wide = nodes * queries
     group = wide if wide <= pad_to(tiles, nodes) else nodes
     held = pad_to(tiles, group)
-    sent, loss = call(
+    sent = call(
         functools.partial(combine_kernel, (q_local, width)),
         "combine",
-        [(held, SUBLANES, LANES), (1, q_local)],
+        [(held, SUBLANES, LANES)],
         10**6,
         all_totals,
         totals,
@@ -549,12 +591,13 @@
         mine = lax.psum(jnp.sum(parts, axis=0), "queries")
         mine = jnp.broadcast_to(mine, (group,) + mine.shape)
     final = swap(mine, axes).reshape(held, SUBLANES, LANES)
-    grad_rel, grad_layer, grad_entity, grad_query, grad_score = call(
+    grad_rel, grad_layer, grad_entity, grad_query, grad_score, loss = call(
         functools.partial(unpack_kernel, (relations, across)),
         "unpack",
-        [(width, relations), (width, width), (width, hid), (width, hid), (1, hid)],
+        [(width, relations), (width, width), (width, hid), (width, hid), (1, hid), (1, q_local)],
         10**6,
         final,
+        all_totals,
     )
     return (
         new_state,

time: 60.6 us -> 56.7 us (0.936)
  local copies, waits for them, and re-layouts: 7.93 us -> 4.97 us
  waiting for transfers between devices: 2.86 us -> 1.06 us
  Pallas kernels: 14.7 us -> 15.4 us
    unnamed x42 -> x38, local copies, waits for them, and re-layouts: 7.93 us -> 4.97 us
    all_to_all x2, waiting for transfers between devices: 2.86 us -> 1.06 us  [swap(): return lax.all_to_all(values, axes, split_axis=0, concat_axis=0, tiled=True)]
    pallas_call x7, Pallas kernels: 14.7 us -> 15.4 us  [call(): pl.pallas_call(kernel, out_shape=tuple((dims if isinstance(dims, jax.Shap...]
  transfers between devices with their start and end apart: 2 -> 2, of which waited for: 1 -> 1; matrix products, arithmetic and copies ran while one was open for 0% -> 0% of each run, Pallas kernels for 11% -> 12%
where the time goes in v1:
time: 56.7 us; the launch traced here: 56.1 us
  blocking collectives  24.6 us (43%)
  Pallas kernels  15.4 us (27%)
  starting transfers between devices  8.52 us (15%)
  local copies, waits for them, and re-layouts  4.97 us (9%)
  between operations  1.5 us (3%)
  waiting for transfers between devices  1.06 us (2%)
    all_to_all x2, blocking collectives, swap(): return lax.all_to_all(values, axes, split_axis=0, concat_axis=0, tiled=True)  24.6 us
    pallas_call x7, Pallas kernels, call(): pl.pallas_call(kernel, out_shape=tuple((dims if isinstance(dims, jax.Shap...  15.4 us
    all_to_all x2, starting transfers between devices, swap(): return lax.all_to_all(values, axes, split_axis=0, concat_axis=0, tiled=True)  8.52 us
    unnamed x38, local copies, waits for them, and re-layouts  4.97 us
  transfers between devices with their start and end apart: 2, of which 1 were waited for; matrix products, arithmetic and copies ran while one was open for 0% of the time, Pallas kernels for 12%

profile of v1, /device:TPU:0, one launch (start us, length us, event | category | flops | bytes accessed | tf_op | source)
XLA Modules:
  0.0 56.1 jit_solution(18082420292889114792)
XLA Ops:
  0.6 2.1 %send.1 = f32[8,64,128]{2,1,0:T(8,128)} custom-call(s32[8,64]{1,0:T(8,128)} %bitcast.31, f32[256,128]{1,0:T(8,128)} %state_ref.3), custom_call_target="tpu_custom_call" | custom-call | flops 1000000000 | bytes 1048576 | tf_op jit(solution)/shard_map/send/pallas_call | solution.py:440
  2.8 5.2 %all-to-all-start = ((f32[8,64,128]{2,1,0:T(8,128)}), f32[8,64,128]{2,1,0:T(8,128)S(1)}, u32[]{:S(2)}, u32[]{:S(2)}) async-start(f32[8,64,128]{2,1,0:T(8,128)} %send.1), calls=%async_computation | async-start | bytes 524288 | tf_op jit(solution)/shard_map/all_to_all | solution.py:458
  8.6 0.0 copy-start
  8.6 0.9 %copy-done = f32[256,128]{1,0:T(8,128)S(1)} copy-done((f32[256,128]{1,0:T(8,128)S(1)}, f32[256,128]{1,0:T(8,128)}, u32[]{:S(2)}) %copy-start) | copy-done | bytes 131096
  9.5 0.9 %copy-done.2 = f32[535,32]{0,1:T(8,128)S(1)} copy-done((f32[535,32]{0,1:T(8,128)S(1)}, f32[535,32]{0,1:T(8,128)}, u32[]{:S(2)}) %copy-start.2) | copy-done | bytes 68504
  10.4 0.7 %copy-done.4 = s32[4096]{0:T(1024)S(1)} copy-done((s32[4096]{0:T(1024)S(1)}, s32[4096]{0:T(1024)}, u32[]{:S(2)}) %copy-start.4) | copy-done | bytes 16408
  11.1 0.7 %copy-done.7 = s32[4096]{0:T(1024)S(1)} copy-done((s32[4096]{0:T(1024)S(1)}, s32[4096]{0:T(1024)}, u32[]{:S(2)}) %copy-start.7) | copy-done | bytes 16408
  11.8 0.0 copy-start.9
  11.8 0.0 copy-start.10
  11.9 0.0 copy-start.13
  11.9 0.0 copy-start.14
  11.9 0.0 copy-start.16
  11.9 1.9 %early.1 = (f32[128,4096]{1,0:T(8,128)S(1)}, f32[32,4096]{1,0:T(8,128)S(1)}) custom-call(f32[256,128]{1,0:T(8,128)S(1)} %copy-done, s32[1,4096]{1,0:T(1,128)S(1)} %bitcast.19, s32[1,4096]{1,0:T(1,128)S(1)} %bitcast.23, f32[32,535]{1,0:T(8,128)S(1)} %bitcast.17), custom_call_target="tpu_custom_call" | custom-call | flops 4000000000 | bytes 1048576 | tf_op jit(solution)/shard_map/early/pallas_call | solution.py:440
  13.8 1.1 %all-to-all-done = f32[8,64,128]{2,1,0:T(8,128)S(1)} async-done(((f32[8,64,128]{2,1,0:T(8,128)}), f32[8,64,128]{2,1,0:T(8,128)S(1)}, u32[]{:S(2)}, u32[]{:S(2)}) %all-to-all-start) | async-done | bytes 262176 | tf_op jit(solution)/shard_map/all_to_all | solution.py:458
  15.0 0.0 copy-start.8
  15.0 4.8 %forward.1 = (f32[256,128]{1,0:T(8,128)}, f32[128,4096]{1,0:T(8,128)S(1)}, f32[128,256]{1,0:T(8,128)S(1)}, bf16[128,256]{1,0:T(8,128)(2,1)S(1)}, f32[104,768]{1,0:T(8,128)S(1)}, /*index=5*/f32[8,8,128]{2,1,0:T(8,128)}) custom-call(s32[1,1]{1,0:T(1,128)} %bitcast.14.count_ref, s32[1,4]{1,0:T(1,128)S(1)} %bitcast.25, ...), custom_call_target="tpu_custom_call", output_to_operand_aliasing={{1}: (9, {})} | custom-call | flops 4000000000 | bytes 1048576 | tf_op jit(solution)/shard_map/forward/pallas_call | solution.py:440
  19.8 0.7 %copy-done.17 = f32[104,768]{1,0:T(8,128)} copy-done((f32[104,768]{1,0:T(8,128)}, f32[104,768]{1,0:T(8,128)S(1)}, u32[]{:S(2)}) %copy-start.17) | copy-done | bytes 319512
  20.6 3.3 %all-to-all-start.1 = ((f32[8,8,128]{2,1,0:T(8,128)}), f32[8,8,128]{2,1,0:T(8,128)S(1)}, u32[]{:S(2)}, u32[]{:S(2)}) async-start(f32[8,8,128]{2,1,0:T(8,128)} %get-tuple-element.24.own_ref), calls=%async_computation.1 | async-start | bytes 65536 | tf_op jit(solution)/shard_map/all_to_all | solution.py:458
  23.9 1.0 %copy-done.18 = f32[104,768]{1,0:T(8,128)S(1)} copy-done((f32[104,768]{1,0:T(8,128)S(1)}, f32[104,768]{1,0:T(8,128)}, u32[]{:S(2)}) %copy-start.18) | copy-done | bytes 319512
  24.9 5.0 %backward.1.grads_ref = f32[160,896]{1,0:T(8,128)S(1)} custom-call(s32[1,1]{1,0:T(1,128)} %bitcast.15.count_ref, f32[128,4096]{1,0:T(8,128)S(1)} %get-tuple-element.25.srct_ref, s32[1,4096]{1,0:T(1,128)S(1)} %bitcast.22, s32[1,4096]{1,0:T(1,128)S(1)} %bitcast.24, f32[32,32]{1,0:T(8,128)S(1)} %copy-done.9, f32[32,64]{1,0:T(8,128)S(1)} %copy-done.10, ...), custom_call_target="tpu_custom_call" | custom-call | flops 4000000000 | bytes 1048576 | tf_op jit(solution)/shard_map/backward/pallas_call | solution.py:440
  29.9 0.9 %combine.1 = f32[32,8,128]{2,1,0:T(8,128)S(1)} custom-call(f32[8,8,128]{2,1,0:T(8,128)S(1)} %all-to-all-done.1.totals_ref, f32[8,8,128]{2,1,0:T(8,128)} %get-tuple-element.24.own_ref, f32[160,896]{1,0:T(8,128)S(1)} %backward.1.grads_ref), custom_call_target="tpu_custom_call" | custom-call | flops 1000000 | bytes 1048576 | tf_op jit(solution)/shard_map/combine/pallas_call | solution.py:440
  30.8 14.4 %all_to_all.20.parts_ref = f32[32,8,128]{2,1,0:T(8,128)S(1)} all-to-all(f32[32,8,128]{2,1,0:T(8,128)S(1)} %combine.1), channel_id=1, replica_groups=mesh['nodes'=8,'queries'=4] {'nodes','queries'}, dimensions={0} | all-to-all | bytes 262144 | tf_op jit(solution)/shard_map/all_to_all | solution.py:458
  45.3 10.1 %all_to_all.21.tiles_ref = f32[32,8,128]{2,1,0:T(8,128)S(1)} all-to-all(f32[32,8,128]{2,1,0:T(8,128)S(1)} %spread.1), channel_id=1, replica_groups=mesh['nodes'=8,'queries'=4] {'nodes','queries'}, dimensions={0} | all-to-all | bytes 262144 | tf_op jit(solution)/shard_map/all_to_all | solution.py:458
  55.4 0.7 %unpack.1 = (f32[32,535]{1,0:T(8,128)}, f32[32,32]{1,0:T(8,128)}, f32[32,64]{1,0:T(8,128)}, f32[32,64]{1,0:T(8,128)}, f32[1,64]{1,0:T(1,128)}, /*index=5*/f32[1,4]{1,0:T(1,128)}) custom-call(f32[32,8,128]{2,1,0:T(8,128)S(1)} %all_to_all.21.tiles_ref, f32[8,8,128]{2,1,0:T(8,128)S(1)} %all-to-all-done.1.totals_ref), custom_call_target="tpu_custom_call" | custom-call | flops 1000000 | bytes 1048576 | tf_op jit(solution)/shard_map/unpack/pallas_call | solution.py:440
  (27 shorter events, 0.1 us)
Async XLA Ops:
  2.8 12.1 %all-to-all-start = ((f32[8,64,128]{2,1,0:T(8,128)}), f32[8,64,128]{2,1,0:T(8,128)S(1)}, u32[]{:S(2)}, u32[]{:S(2)}) async-start(f32[8,64,128]{2,1,0:T(8,128)} %send.1), calls=%async_computation | async-start | bytes 524288 | tf_op jit(solution)/shard_map/all_to_all | solution.py:458
  8.6 0.9 %copy-start = (f32[256,128]{1,0:T(8,128)S(1)}, f32[256,128]{1,0:T(8,128)}, u32[]{:S(2)}) copy-start(f32[256,128]{1,0:T(8,128)} %state_ref.3) | copy-start | bytes 393220
  9.5 0.9 %copy-start.2 = (f32[535,32]{0,1:T(8,128)S(1)}, f32[535,32]{0,1:T(8,128)}, u32[]{:S(2)}) copy-start(f32[535,32]{0,1:T(8,128)} %param.25) | copy-start | bytes 205444
  10.4 0.7 %copy-start.4 = (s32[4096]{0:T(1024)S(1)}, s32[4096]{0:T(1024)}, u32[]{:S(2)}) copy-start(s32[4096]{0:T(1024)} %param.16) | copy-start | bytes 49156
  11.1 0.7 %copy-start.7 = (s32[4096]{0:T(1024)S(1)}, s32[4096]{0:T(1024)}, u32[]{:S(2)}) copy-start(s32[4096]{0:T(1024)} %param.18) | copy-start | bytes 49156
  11.8 3.1 %copy-start.1 = (f32[256,128]{1,0:T(8,128)S(1)}, f32[256,128]{1,0:T(8,128)}, u32[]{:S(2)}) copy-start(f32[256,128]{1,0:T(8,128)} %state_ref.3) | copy-start | bytes 393220
  11.8 3.1 %copy-start.3 = (f32[535,32]{0,1:T(8,128)S(1)}, f32[535,32]{0,1:T(8,128)}, u32[]{:S(2)}) copy-start(f32[535,32]{0,1:T(8,128)} %param.25) | copy-start | bytes 205444
  11.8 3.1 %copy-start.5 = (s32[4096]{0:T(1024)S(1)}, s32[4096]{0:T(1024)}, u32[]{:S(2)}) copy-start(s32[4096]{0:T(1024)} %param.16) | copy-start | bytes 49156
  11.8 3.1 %copy-start.6 = (s32[4096]{0:T(1024)S(1)}, s32[4096]{0:T(1024)}, u32[]{:S(2)}) copy-start(s32[4096]{0:T(1024)} %param.17) | copy-start | bytes 49156
  11.8 3.1 %copy-start.9 = (f32[32,32]{1,0:T(8,128)S(1)}, f32[32,32]{1,0:T(8,128)}, u32[]{:S(2)}) copy-start(f32[32,32]{1,0:T(8,128)} %layer_ref.3) | copy-start | bytes 12292
  11.8 3.1 %copy-start.10 = (f32[32,64]{1,0:T(8,128)S(1)}, f32[32,64]{1,0:T(8,128)}, u32[]{:S(2)}) copy-start(f32[32,64]{1,0:T(8,128)} %ment_ref.3) | copy-start | bytes 24580
  11.9 3.1 %copy-start.11 = (f32[32,64]{1,0:T(8,128)S(1)}, f32[32,64]{1,0:T(8,128)}, u32[]{:S(2)}) copy-start(f32[32,64]{1,0:T(8,128)} %mquery_ref.3) | copy-start | bytes 24580
  11.9 3.1 %copy-start.12 = (s32[4,128]{1,0:T(4,128)S(1)}, s32[4,128]{1,0:T(4,128)}, u32[]{:S(2)}) copy-start(s32[4,128]{1,0:T(4,128)} %neg_ref.1) | copy-start | bytes 6148
  11.9 3.1 %copy-start.13 = (s32[4]{0:T(128)S(1)}, s32[4]{0:T(128)}, u32[]{:S(2)}) copy-start(s32[4]{0:T(128)} %param.21) | copy-start | bytes 52
  11.9 3.1 %copy-start.14 = (s32[4]{0:T(128)S(1)}, s32[4]{0:T(128)}, u32[]{:S(2)}) copy-start(s32[4]{0:T(128)} %param.22) | copy-start | bytes 52
  11.9 3.1 %copy-start.15 = (s32[4]{0:T(128)S(1)}, s32[4]{0:T(128)}, u32[]{:S(2)}) copy-start(s32[4]{0:T(128)} %param.23) | copy-start | bytes 52
  11.9 3.1 %copy-start.16 = (f32[64]{0:T(128)S(1)}, f32[64]{0:T(128)}, u32[]{:S(2)}) copy-start(f32[64]{0:T(128)} %param.29) | copy-start | bytes 772
  15.0 8.9 %copy-start.8 = (s32[4096]{0:T(1024)S(1)}, s32[4096]{0:T(1024)}, u32[]{:S(2)}) copy-start(s32[4096]{0:T(1024)} %param.18) | copy-start | bytes 49156
  19.8 0.7 %copy-start.17 = (f32[104,768]{1,0:T(8,128)}, f32[104,768]{1,0:T(8,128)S(1)}, u32[]{:S(2)}) copy-start(f32[104,768]{1,0:T(8,128)S(1)} %get-tuple-element.28.columns_ref) | copy-start | bytes 958468
  20.6 9.3 %all-to-all-start.1 = ((f32[8,8,128]{2,1,0:T(8,128)}), f32[8,8,128]{2,1,0:T(8,128)S(1)}, u32[]{:S(2)}, u32[]{:S(2)}) async-start(f32[8,8,128]{2,1,0:T(8,128)} %get-tuple-element.24.own_ref), calls=%async_computation.1 | async-start | bytes 65536 | tf_op jit(solution)/shard_map/all_to_all | solution.py:458
  23.9 1.0 %copy-start.18 = (f32[104,768]{1,0:T(8,128)S(1)}, f32[104,768]{1,0:T(8,128)}, u32[]{:S(2)}) copy-start(f32[104,768]{1,0:T(8,128)} %copy-done.17) | copy-start | bytes 958468

commit v2 on v1

v2 whole, which is shorter than its diff:
```python
import functools

import jax
import jax.numpy as jnp
from jax import lax
from jax.experimental import pallas as pl
from jax.experimental.pallas import tpu as pltpu
from jax.sharding import PartitionSpec as P

adversarial = 0.5
HIGH = lax.Precision.HIGHEST
F32 = jnp.float32
BF16 = jnp.bfloat16
LANES = 128
SUBLANES = 8
FORWARD = 3
BACKWARD = 2
SEND_LIMIT = 64 << 20


def pad_to(count, unit):
    return -(-count // unit) * unit


def split(values, pieces, axis=0):
    found = []
    for _ in range(pieces):
        piece = values.astype(BF16)
        values = values - piece.astype(F32)
        found.append(piece)
    return jnp.concatenate(found, axis=axis)


def join(values, pieces, axis=0):
    size = values.shape[axis] // pieces
    parts = [
        lax.slice_in_dim(values, piece * size, (piece + 1) * size, axis=axis)
        for piece in range(pieces)
    ]
    return functools.reduce(jnp.add, parts)


def one_hot(index_row, rows):
    parts = []
    for base in range(0, rows, 256):
        size = min(256, rows - base)
        local = index_row - base
        key = jnp.where((local >= 0) & (local < size), local, -1).astype(F32).astype(BF16)
        spots = lax.broadcasted_iota(jnp.int32, (size, index_row.shape[1]), 0)
        same = spots.astype(F32).astype(BF16) == key
        parts.append(jnp.where(same, jnp.ones((), BF16), jnp.zeros((), BF16)))
    return parts[0] if len(parts) == 1 else jnp.concatenate(parts, axis=0)


def dot_nn(left, right, precision=None):
    return lax.dot_general(
        left, right, (((1,), (0,)), ((), ())), precision=precision, preferred_element_type=F32
    )


def dot_nt(left, right, precision=None):
    return lax.dot_general(
        left, right, (((1,), (1,)), ((), ())), precision=precision, preferred_element_type=F32
    )


def pieces_of(values, count):
    found = []
    for _ in range(count):
        piece = values.astype(BF16)
        values = values - piece.astype(F32)
        found.append(piece)
    return found


LEFT = {6: (0, 0, 1, 0, 2, 1), 3: (0, 0, 1)}
RIGHT = {6: (0, 1, 0, 2, 0, 1), 3: (0, 1, 0)}


def stack_left(values, terms, axis=1):
    pieces = pieces_of(values, max(LEFT[terms]) + 1)
    return jnp.concatenate([pieces[spot] for spot in LEFT[terms]], axis=axis)


def stack_right(values, terms, axis=0):
    pieces = pieces_of(values, max(RIGHT[terms]) + 1)
    return jnp.concatenate([pieces[spot] for spot in RIGHT[terms]], axis=axis)


def local_row(entity, ent_local):
    node = lax.axis_index("nodes")
    return jnp.where(entity // ent_local == node, entity % ent_local, -1)


def in_lanes(small_row):
    lane = lax.broadcasted_iota(jnp.int32, (1, LANES), 1)
    found = jnp.full((1, LANES), -1, jnp.int32)
    for spot in range(small_row.shape[1]):
        found = jnp.where(lane == spot, small_row[:, spot : spot + 1], found)
    return found


def as_column(row):
    size = row.shape[1]
    across = lax.broadcasted_iota(jnp.int32, (size, size), 1)
    down = lax.broadcasted_iota(jnp.int32, (size, size), 0)
    return jnp.sum(jnp.where(across == down, row, 0.0), axis=1, keepdims=True)


def as_row(column):
    size = column.shape[0]
    across = lax.broadcasted_iota(jnp.int32, (size, size), 1)
    down = lax.broadcasted_iota(jnp.int32, (size, size), 0)
    return jnp.sum(jnp.where(across == down, column, 0.0), axis=0, keepdims=True)


def fill_rows(rows, count):
    missing = count - len(rows)
    return jnp.concatenate(rows + [jnp.zeros((missing,) + rows[0].shape[1:], rows[0].dtype)], axis=0)


def kept_layout(q_local, ent, neg, parts=2):
    columns = q_local * neg + LANES
    ends = [0, q_local * ent] + [q_local * ent + (part + 1) * columns for part in range(1 + parts)]
    return [slice(low, high) for low, high in zip(ends, ends[1:])]


def send_kernel(send_ref, state_ref, out_ref):
    count, bound = send_ref.shape
    ent = state_ref.shape[0]
    pieces = split(state_ref[...], FORWARD, axis=1)
    wanted = send_ref[...].T
    entity = lax.broadcasted_iota(jnp.int32, (bound, ent), 1)
    for n in range(count):
        hot = (entity == wanted[:, n : n + 1]).astype(F32).astype(BF16)
        out_ref[n] = join(dot_nn(hot, pieces), FORWARD, axis=1)


def early_kernel(
    sizes,
    state_ref,
    src_ref,
    rel_ref,
    table_ref,
    head_ref,
    qrel_ref,
    tail_ref,
    layer_ref,
    ment_ref,
    mquery_ref,
    score_ref,
    local_ref,
    relation_ref,
    prep_ref,
    marks_ref,
):
    (chunk,) = sizes
    ent = state_ref.shape[0]
    width, relations = table_ref.shape
    hid = ment_ref.shape[1]
    edges = src_ref.shape[1]
    rel_rows = pad_to(relations, 16)
    state_bits = split(state_ref[...].T, FORWARD)
    rel_bits = split(table_ref[...], FORWARD)
    rel_bits = jnp.concatenate(
        [rel_bits, jnp.zeros((FORWARD * width, rel_rows - relations), BF16)], axis=1
    )
    for start in range(0, edges, chunk):
        span = slice(start, start + chunk)
        local_ref[:, span] = join(dot_nn(state_bits, one_hot(src_ref[:, span], ent)), FORWARD)
        relation_ref[:, span] = join(
            dot_nn(rel_bits, one_hot(rel_ref[:, span], rel_rows)), FORWARD
        )
    heads = in_lanes(local_row(head_ref[...], ent))
    tails = in_lanes(local_row(tail_ref[...], ent))
    qrels = in_lanes(qrel_ref[...])
    marks_ref[...] = fill_rows([heads, tails, qrels], SUBLANES)
    qvec = join(dot_nn(rel_bits, one_hot(qrels, rel_rows)), FORWARD)
    prep_ref[:width, :] = qvec
    prep_ref[width : width + hid, :] = dot_nn(mquery_ref[...].T, qvec, HIGH)
    prep_ref[width + hid :, :] = jnp.broadcast_to(as_column(score_ref[...]), (hid, LANES))


def forward_kernel(
    sizes,
    count_ref,
    state_ref,
    recv_ref,
    src_ref,
    dst_ref,
    neg_ref,
    local_ref,
    relation_ref,
    prep_ref,
    marks_ref,
    layer_ref,
    ment_ref,
    new_ref,
    srct_ref,
    kept_ref,
    gate_ref,
    coef_ref,
    totals_ref,
):
    chunk, queries_total = sizes
    ent, blocks = state_ref.shape
    edges = src_ref.shape[1]
    width, hid = ment_ref.shape
    q_local, neg = neg_ref.shape
    per_query = neg // LANES
    layout = kept_layout(q_local, ent, neg)
    recv_bits = split(recv_ref[...].T, FORWARD)
    live = count_ref[...]
    total = jnp.zeros((FORWARD * blocks, ent), F32)
    for start in range(0, edges, chunk):
        span = slice(start, start + chunk)
        far = one_hot(src_ref[:, span] - ent, recv_bits.shape[1])
        source = local_ref[:, span] + join(dot_nn(recv_bits, far), FORWARD)
        srct_ref[:, span] = source
        message = source * jnp.concatenate([relation_ref[:, span]] * q_local, axis=0)
        spot = lax.broadcasted_iota(jnp.int32, (1, chunk), 1) + start
        ends = jnp.where(spot < live, dst_ref[:, span], -1)
        total = total + dot_nt(split(message, FORWARD), one_hot(ends, ent))
    summed = join(total, FORWARD)

    entity_row = lax.broadcasted_iota(jnp.int32, (1, ent), 1)
    lane_row = lax.broadcasted_iota(jnp.int32, (1, LANES), 1)
    heads = marks_ref[0:1, :]
    tails = marks_ref[1:2, :]
    parts = []
    for q in range(q_local):
        at_head = (entity_row == heads[:, q : q + 1]).astype(F32)
        parts.append(summed[q * width : (q + 1) * width] + prep_ref[:width, q : q + 1] * at_head)
    wide = jnp.concatenate(parts, axis=1)
    kept_ref[:, layout[0]] = wide
    pre = dot_nn(stack_left(layer_ref[...].T, 6), stack_right(wide, 6))
    state_t = state_ref[...].T
    new_parts, picks, positive = [], [], None
    for q in range(q_local):
        rows = slice(q * width, (q + 1) * width)
        mine = pre[:, q * ent : (q + 1) * ent]
        gate_ref[rows, :] = (mine > 0.0).astype(F32).astype(BF16)
        new = state_t[rows] + jnp.maximum(mine, 0.0)
        new_parts.append(new)
        own_tail = jnp.where(lane_row == q, tails, -1)
        hot = one_hot(jnp.concatenate([neg_ref[q : q + 1, :], own_tail], axis=1), ent)
        picked = join(dot_nn(split(new, FORWARD), hot), FORWARD)
        picks.append(picked[:, :neg])
        last = picked[:, neg:]
        positive = last if positive is None else positive + last
    new_ref[...] = jnp.concatenate(new_parts, axis=0).T
    picked = jnp.concatenate(picks + [positive], axis=1)
    kept_ref[:, layout[1]] = picked
    plain = dot_nn(stack_left(ment_ref[...].T, 6), stack_right(picked, 6))
    rows = []
    for block in range(plain.shape[1] // LANES):
        span = slice(block * LANES, (block + 1) * LANES)
        q = block // per_query
        part = prep_ref[width : width + hid, :]
        if q < q_local:
            part = part[:, q : q + 1]
        hidden = plain[:, span] + part
        for part in range(hid // width):
            left = layout[2 + part].start + block * LANES
            kept_ref[:, left : left + LANES] = hidden[part * width : (part + 1) * width]
        weighted = jnp.maximum(hidden, 0.0) * prep_ref[width + hid :, :]
        rows.append(jnp.sum(weighted, axis=0, keepdims=True))
    height = coef_ref.shape[0]
    scores = fill_rows(rows, height)
    weights = jnp.exp(adversarial * scores)
    decay = jnp.exp(-jnp.abs(scores))
    near = jnp.log1p(decay)
    softplus = jnp.maximum(scores, 0.0) + near
    flipped = jnp.maximum(-scores, 0.0) + near
    share = 1.0 / (1.0 + decay)
    sigmoid = jnp.where(scores >= 0.0, share, decay * share)
    missing = jnp.where(scores >= 0.0, decay * share, share)
    row_total = jnp.sum(weights, axis=1, keepdims=True)
    row_weighted = jnp.sum(weights * softplus, axis=1, keepdims=True)
    present = (tails >= 0) & (lane_row < q_local)
    tail_row = len(rows) - 1
    positives = jnp.where(present, flipped[tail_row : tail_row + 1], 0.0)
    owns, weighteds, row_owns = [], [], []
    for q in range(q_local):
        mine = slice(q * per_query, (q + 1) * per_query)
        own = jnp.sum(row_total[mine], axis=0, keepdims=True)
        owns.append(own)
        row_owns.extend([own] * per_query)
        weighteds.append(jnp.sum(row_weighted[mine], axis=0, keepdims=True))
    row_own = fill_rows(row_owns, height)
    coef = weights * sigmoid / jnp.where(row_own > 0.0, row_own, 1.0)
    spot = lax.broadcasted_iota(jnp.int32, (height, LANES), 0)
    coef = jnp.where(spot < tail_row, coef, 0.0)
    coef = jnp.where((spot == tail_row) & present, -missing, coef)
    coef_ref[...] = coef * (1.0 / queries_total)
    tall = totals_ref.shape[1]
    pair = jnp.where(
        lax.broadcasted_iota(jnp.int32, (tall, LANES), 1) == 0,
        fill_rows(owns, tall),
        fill_rows(weighteds, tall),
    )
    down = lax.broadcasted_iota(jnp.int32, (tall, LANES), 0)
    tile = jnp.where(down == tall - 1, positives, pair)
    for n in range(totals_ref.shape[0]):
        totals_ref[n] = tile


def backward_kernel(
    sizes,
    count_ref,
    srct_ref,
    dst_ref,
    rel_ref,
    neg_ref,
    prep_ref,
    marks_ref,
    layer_ref,
    ment_ref,
    mquery_ref,
    kept_ref,
    gate_ref,
    coef_ref,
    out_ref,
):
    chunk, relations = sizes
    width, hid = ment_ref.shape
    blocks, ent = gate_ref.shape
    q_local, neg = neg_ref.shape
    edges = dst_ref.shape[1]
    layout = kept_layout(q_local, ent, neg)
    picked = kept_ref[:, layout[1]]
    hidden = jnp.concatenate([kept_ref[:, spot] for spot in layout[2:]], axis=0)
    per_query = neg // LANES
    rel_lanes = pad_to(relations, LANES)
    rel_rows = pad_to(relations, 16)
    heads = marks_ref[0:1, :]
    tails = marks_ref[1:2, :]
    qrels = marks_ref[2:3, :]
    entity_row = lax.broadcasted_iota(jnp.int32, (1, ent), 1)
    rel_row = lax.broadcasted_iota(jnp.int32, (1, rel_lanes), 1)
    grad_parts, coef_parts = [], []
    for block in range(hidden.shape[1] // LANES):
        span = slice(block * LANES, (block + 1) * LANES)
        coef = coef_ref[block : block + 1, :]
        coef_parts.append(coef)
        grad_parts.append(
            jnp.where(hidden[:, span] > 0.0, coef * prep_ref[width + hid :, :], 0.0)
        )
    grad_hidden = jnp.concatenate(grad_parts, axis=1)
    both = jnp.concatenate([ment_ref[...], mquery_ref[...]], axis=0)
    grad_both = dot_nn(stack_left(both, 3), stack_right(grad_hidden, 3))
    last = q_local * neg
    pres, tail_pres = [], []
    for q in range(q_local):
        rows = slice(q * width, (q + 1) * width)
        span = slice(q * neg, (q + 1) * neg)
        gate = gate_ref[rows, :].astype(F32)
        hot = one_hot(neg_ref[q : q + 1, :], ent)
        cube = join(dot_nt(split(grad_both[:width, span], BACKWARD), hot), BACKWARD)
        pres.append(gate * cube)
        at_tail = (entity_row == tails[:, q : q + 1]).astype(F32)
        tail_pres.append(gate * (grad_both[:width, last + q : last + q + 1] * at_tail))
    stacked = stack_right(jnp.concatenate(pres + tail_pres, axis=1), 3)
    sums = dot_nn(stack_left(layer_ref[...], 3), stacked)
    grad_sums = [sums[:, q * ent : (q + 1) * ent] for q in range(2 * q_local)]
    sum_bits = split(jnp.concatenate(grad_sums[:q_local], axis=0), BACKWARD)
    tail_columns = [
        jnp.sum(grad_sums[q_local + q], axis=1, keepdims=True) for q in range(q_local)
    ]

    live = count_ref[...]
    total = jnp.zeros((BACKWARD * (blocks + width), rel_rows), F32)
    for start in range(0, edges, chunk):
        span = slice(start, start + chunk)
        spot = lax.broadcasted_iota(jnp.int32, (1, chunk), 1) + start
        ends = jnp.where(spot < live, dst_ref[:, span], -2)
        source = srct_ref[:, span]
        upstream = join(dot_nn(sum_bits, one_hot(ends, ent)), BACKWARD)
        tail_terms = jnp.zeros((width, chunk), F32)
        for q in range(q_local):
            rows = slice(q * width, (q + 1) * width)
            hit = (ends == tails[:, q : q + 1]).astype(F32)
            tail_terms = tail_terms + (tail_columns[q] * hit) * source[rows]
        terms = jnp.concatenate([upstream * source, tail_terms], axis=0)
        total = total + dot_nt(split(terms, BACKWARD), one_hot(rel_ref[:, span], rel_rows))
    gathered = join(total, BACKWARD)
    if rel_lanes > rel_rows:
        gathered = jnp.concatenate(
            [gathered, jnp.zeros((blocks + width, rel_lanes - rel_rows), F32)], axis=1
        )

    seeds = []
    tail_seed = jnp.zeros((width, rel_lanes), F32)
    tail_layer = jnp.zeros((width, width), F32)
    spare = jnp.zeros((width, out_ref.shape[1] - rel_lanes - width - 3 * hid), F32)
    for block in range(q_local + 1):
        if block < q_local:
            q = block
            rows = slice(q * width, (q + 1) * width)
            span = slice(q * neg, (q + 1) * neg)
            at_head = (entity_row == heads[:, q : q + 1]).astype(F32)
            at_rel = (rel_row == qrels[:, q : q + 1]).astype(F32)
            grad_qvec = jnp.sum(grad_both[width:, span], axis=1, keepdims=True) + jnp.sum(
                grad_sums[q] * at_head, axis=1, keepdims=True
            )
            seeds.append(grad_qvec * at_rel)
            tail_qvec = grad_both[width:, last + q : last + q + 1] + jnp.sum(
                grad_sums[q_local + q] * at_head, axis=1, keepdims=True
            )
            tail_seed = tail_seed + tail_qvec * at_rel
            left = stack_left(kept_ref[:, q * ent : (q + 1) * ent], 3)
            right = jnp.concatenate(
                [stack_right(pres[q], 3, axis=1), stack_right(tail_pres[q], 3, axis=1)], axis=0
            )
            layers = dot_nt(left, right)
            layer_part = layers[:, :width]
            tail_layer = tail_layer + layers[:, width:]
            vectors = jnp.broadcast_to(prep_ref[:width, q : q + 1], (width, neg))
            coef_rows = coef_parts[q * per_query : (q + 1) * per_query]
        else:
            span = slice(last, last + LANES)
            layer_part = tail_layer
            vectors = prep_ref[:width, :]
            coef_rows = coef_parts[-1:]
        size = span.stop - span.start
        coef = jnp.broadcast_to(jnp.concatenate(coef_rows, axis=1), (width, size))
        right = jnp.concatenate([grad_hidden[:, span], jnp.maximum(hidden[:, span], 0.0)], axis=0)
        right = stack_right(right, 3, axis=1)
        entity_part = dot_nt(stack_left(picked[:, span], 3), right)[:, :hid]
        query_part = dot_nt(stack_left(vectors, 3), right)[:, :hid]
        score_part = dot_nt(stack_left(coef, 3), right)[:, hid:]
        rest = [layer_part, entity_part, query_part, score_part, spare]
        out_ref[block * width : (block + 1) * width, rel_lanes:] = jnp.concatenate(rest, axis=1)
    seeds.append(tail_seed)
    out_ref[:, :rel_lanes] = gathered + jnp.concatenate(seeds, axis=0)


def combine_kernel(sizes, totals_ref, grads_ref, sent_ref):
    q_local, width = sizes
    total = jnp.sum(totals_ref[...], axis=0)
    scale = totals_ref[lax.axis_index("nodes")] / total
    mixed = grads_ref[q_local * width :, :]
    for q in range(q_local):
        mixed = mixed + grads_ref[q * width : (q + 1) * width, :] * scale[q : q + 1, 0:1]
    across = mixed.shape[1] // LANES
    tiles = width // SUBLANES * across
    for tile in range(tiles):
        top, left = tile // across * SUBLANES, tile % across * LANES
        sent_ref[tile] = mixed[top : top + SUBLANES, left : left + LANES]
    for tile in range(tiles, sent_ref.shape[0]):
        sent_ref[tile] = jnp.zeros((SUBLANES, LANES), F32)


def spread_kernel(parts_ref, out_ref):
    total = jnp.sum(parts_ref[...], axis=0)
    for n in range(out_ref.shape[0]):
        out_ref[n] = total


def unpack_kernel(
    sizes, tiles_ref, totals_ref, rel_ref, layer_ref, ment_ref, mquery_ref, score_ref, loss_ref
):
    relations, across = sizes
    width, hid = ment_ref.shape
    down = width // SUBLANES
    flat = jnp.concatenate(
        [
            jnp.concatenate([tiles_ref[row * across + tile] for tile in range(across)], axis=1)
            for row in range(down)
        ],
        axis=0,
    )
    rel_lanes = pad_to(relations, LANES)
    rel_ref[...] = flat[:, :relations]
    start = rel_lanes
    layer_ref[...] = flat[:, start : start + width]
    start += width
    ment_ref[...] = flat[:, start : start + hid]
    start += hid
    mquery_ref[...] = flat[:, start : start + hid]
    start += hid
    score_ref[...] = flat[0:1, start : start + hid]
    everyone = jnp.sum(totals_ref[...], axis=0)
    count = loss_ref.shape[1]
    ratio = as_row(everyone[:count, 1:2] / everyone[:count, 0:1])
    loss_ref[...] = everyone[-1:, :count] + ratio


def call(kernel, name, outs, flops, *operands, scratch=(), limit=40 << 20, far=(), alias=None):
    spaces = [pltpu.HBM if spot in far else pltpu.VMEM for spot in range(len(operands))]
    found = pl.pallas_call(
        kernel,
        out_shape=tuple(
            dims if isinstance(dims, jax.ShapeDtypeStruct) else jax.ShapeDtypeStruct(dims, F32)
            for dims in outs
        ),
        in_specs=[pl.BlockSpec(memory_space=space) for space in spaces],
        out_specs=tuple(pl.BlockSpec(memory_space=pltpu.VMEM) for _ in outs),
        scratch_shapes=scratch,
        input_output_aliases=alias or {},
        compiler_params=pltpu.CompilerParams(vmem_limit_bytes=limit),
        cost_estimate=pl.CostEstimate(flops=flops, bytes_accessed=1 << 20, transcendentals=0),
        name=name,
    )(*operands)
    return found[0] if len(outs) == 1 else found


def swap(values, axes):
    return lax.all_to_all(values, axes, split_axis=0, concat_axis=0, tiled=True)


def body(
    state_in,
    edge_src,
    edge_dst,
    edge_rel,
    edge_count,
    send_list,
    query_head,
    query_rel,
    pos_tail,
    neg_ids,
    rel_table,
    layer_weight,
    mlp_entity,
    mlp_query,
    score_weight,
):
    nodes = lax.axis_size("nodes")
    queries = lax.axis_size("queries")
    ent, width_all = state_in.shape
    relations, width = rel_table.shape
    hid = mlp_entity.shape[1]
    q_local = width_all // width
    edges = edge_src.shape[0]
    bound = send_list.shape[2]
    neg = neg_ids.shape[1]
    columns = q_local * neg + LANES
    chunk = min(1024, edges)
    src_row = edge_src.reshape(1, edges)
    dst_row = edge_dst.reshape(1, edges)
    rel_row = edge_rel.reshape(1, edges)
    count = edge_count.reshape(1, 1)
    score_row = score_weight.reshape(1, hid)
    table_t = rel_table.T
    outgoing = call(
        send_kernel, "send", [(nodes, bound, width_all)], 10**9, send_list[0], state_in
    )
    received = swap(outgoing, "nodes").reshape(nodes * bound, width_all)
    local, relation, prep, marks = call(
        functools.partial(early_kernel, (chunk,)),
        "early",
        [
            (width_all, edges),
            (width, edges),
            (width + 2 * hid, LANES),
            jax.ShapeDtypeStruct((SUBLANES, LANES), jnp.int32),
        ],
        4 * 10**9,
        state_in,
        src_row,
        rel_row,
        table_t,
        query_head.reshape(1, q_local),
        query_rel.reshape(1, q_local),
        pos_tail.reshape(1, q_local),
        layer_weight,
        mlp_entity,
        mlp_query,
        score_row,
    )
    needed = kept_layout(q_local, ent, neg)[-1].stop
    new_state, source_t, kept, gate, coef, totals = call(
        functools.partial(forward_kernel, (chunk, q_local * queries)),
        "forward",
        [
            (ent, width_all),
            (width_all, edges),
            (width, max(needed, edges)),
            jax.ShapeDtypeStruct((width_all, ent), BF16),
            (pad_to(columns // LANES, SUBLANES), LANES),
            (nodes, pad_to(q_local + 1, SUBLANES), LANES),
        ],
        4 * 10**9,
        count,
        state_in,
        received,
        src_row,
        dst_row,
        neg_ids,
        local,
        relation,
        prep,
        marks,
        layer_weight,
        mlp_entity,
        alias={6: 1, 7: 2} if needed <= edges else {6: 1},
    )
    all_totals = swap(totals, "nodes")
    rel_lanes = pad_to(relations, LANES)
    lanes = rel_lanes + pad_to(width + 3 * hid, LANES)
    across = lanes // LANES
    grads = call(
        functools.partial(backward_kernel, (chunk, relations)),
        "backward",
        [((q_local + 1) * width, lanes)],
        4 * 10**9,
        count,
        source_t,
        dst_row,
        rel_row,
        neg_ids,
        prep,
        marks,
        layer_weight,
        mlp_entity,
        mlp_query,
        kept,
        gate,
        coef,
    )
    tiles = width // SUBLANES * across
    wide = nodes * queries
    group = wide if wide <= pad_to(tiles, nodes) else nodes
    held = pad_to(tiles, group)
    sent = call(
        functools.partial(combine_kernel, (q_local, width)),
        "combine",
        [(held, SUBLANES, LANES)],
        10**6,
        all_totals,
        grads,
    )
    axes = ("nodes", "queries") if group == wide else "nodes"
    own = held // group
    parts = swap(sent, axes).reshape(group, own * SUBLANES, LANES)
    if group == wide:
        mine = call(spread_kernel, "spread", [(group, own * SUBLANES, LANES)], 10**6, parts)
    else:
        mine = lax.psum(jnp.sum(parts, axis=0), "queries")
        mine = jnp.broadcast_to(mine, (group,) + mine.shape)
    final = swap(mine, axes).reshape(held, SUBLANES, LANES)
    grad_rel, grad_layer, grad_entity, grad_query, grad_score, loss = call(
        functools.partial(unpack_kernel, (relations, across)),
        "unpack",
        [(width, relations), (width, width), (width, hid), (width, hid), (1, hid), (1, q_local)],
        10**6,
        final,
        all_totals,
    )
    return (
        new_state,
        loss.reshape(q_local),
        grad_rel.T,
        grad_layer,
        grad_entity,
        grad_query,
        grad_score.reshape(hid),
    )


def solution(mesh):
    in_specs = (
        P("nodes", "queries"),
        P("nodes"),
        P("nodes"),
        P("nodes"),
        P("nodes"),
        P("nodes", None, None),
        P("queries"),
        P("queries"),
        P("queries"),
        P("queries", "nodes"),
        P(),
        P(),
        P(),
        P(),
        P(),
    )
    out_specs = (P("nodes", "queries"), P("queries"), P(), P(), P(), P(), P())
    return jax.shard_map(body, mesh=mesh, in_specs=in_specs, out_specs=out_specs, check_vma=False)
```

time: 56.7 us -> 53.2 us (0.938)
  waiting for transfers between devices: 1.06 us -> 4.82 us
  local copies, waits for them, and re-layouts: 4.97 us -> 1.64 us
  Pallas kernels: 15.4 us -> 12.6 us
  blocking collectives: 24.6 us -> 23.8 us
    all_to_all x2, waiting for transfers between devices: 1.06 us -> 4.82 us  [swap(): return lax.all_to_all(values, axes, split_axis=0, concat_axis=0, tiled=True)]
    unnamed x38 -> x30, local copies, waits for them, and re-layouts: 4.97 us -> 1.64 us
    pallas_call x7, Pallas kernels: 15.4 us -> 12.6 us  [call(): pl.pallas_call(kernel, out_shape=tuple((dims if isinstance(dims, jax.Shap...]
    all_to_all x2, blocking collectives: 24.6 us -> 23.8 us  [swap(): return lax.all_to_all(values, axes, split_axis=0, concat_axis=0, tiled=True)]
  transfers between devices with their start and end apart: 2 -> 2, of which waited for: 1 -> 2; matrix products, arithmetic and copies ran while one was open for 0% -> 0% of each run, Pallas kernels for 12% -> 12%
where the time goes in v2:
time: 53.2 us; the launch traced here: 52.8 us
  blocking collectives  23.8 us (45%)
  Pallas kernels  12.6 us (24%)
  starting transfers between devices  8.51 us (16%)
  waiting for transfers between devices  4.82 us (9%)
  local copies, waits for them, and re-layouts  1.64 us (3%)
  between operations  1.48 us (3%)
    all_to_all x2, blocking collectives, swap(): return lax.all_to_all(values, axes, split_axis=0, concat_axis=0, tiled=True)  23.8 us
    pallas_call x7, Pallas kernels, call(): pl.pallas_call(kernel, out_shape=tuple((dims if isinstance(dims, jax.Shap...  12.6 us
    all_to_all x2, starting transfers between devices, swap(): return lax.all_to_all(values, axes, split_axis=0, concat_axis=0, tiled=True)  8.51 us
    all_to_all x2, waiting for transfers between devices, swap(): return lax.all_to_all(values, axes, split_axis=0, concat_axis=0, tiled=True)  4.82 us
    unnamed x30, local copies, waits for them, and re-layouts  1.64 us
  transfers between devices with their start and end apart: 2, of which 2 were waited for; matrix products, arithmetic and copies ran while one was open for 0% of the time, Pallas kernels for 12%

profile of v2, /device:TPU:0, one launch (start us, length us, event | category | flops | bytes accessed | tf_op | source)
XLA Modules:
  0.0 52.8 jit_solution(1315881349860197596)
XLA Ops:
  0.6 0.9 %copy-done = f32[256,128]{1,0:T(8,128)S(1)} copy-done((f32[256,128]{1,0:T(8,128)S(1)}, f32[256,128]{1,0:T(8,128)}, u32[]{:S(2)}) %copy-start) | copy-done | bytes 131096
  1.5 0.7 %copy-done.9 = s32[1,8,64]{2,1,0:T(8,128)S(1)} copy-done((s32[1,8,64]{2,1,0:T(8,128)S(1)}, s32[1,8,64]{2,1,0:T(8,128)}, u32[]{:S(2)}) %copy-start.9) | copy-done | bytes 2072
  2.2 0.0 copy-start.6
  2.3 0.0 copy-start.7
  2.3 0.0 copy-start.8
  2.3 0.0 copy-start.11
  2.3 0.0 copy-start.12
  2.3 0.0 copy-start.13
  2.3 0.0 copy-start.14
  2.3 1.2 %send.1 = f32[8,64,128]{2,1,0:T(8,128)} custom-call(s32[8,64]{1,0:T(8,128)S(1)} %bitcast.24, f32[256,128]{1,0:T(8,128)S(1)} %copy-done), custom_call_target="tpu_custom_call" | custom-call | flops 1000000000 | bytes 1048576 | tf_op jit(solution)/shard_map/send/pallas_call | solution.py:491
  3.5 5.2 %all-to-all-start = ((f32[8,64,128]{2,1,0:T(8,128)}), f32[8,64,128]{2,1,0:T(8,128)S(1)}, u32[]{:S(2)}, u32[]{:S(2)}) async-start(f32[8,64,128]{2,1,0:T(8,128)} %send.1), calls=%async_computation | async-start | bytes 524288 | tf_op jit(solution)/shard_map/all_to_all | solution.py:509
  9.4 0.0 copy-start.4
  9.4 0.0 copy-start.10
  9.4 2.1 %early.1 = (f32[128,4096]{1,0:T(8,128)S(1)}, f32[32,4096]{1,0:T(8,128)S(1)}, f32[160,128]{1,0:T(8,128)S(1)}, s32[8,128]{1,0:T(8,128)S(1)}) custom-call(f32[256,128]{1,0:T(8,128)S(1)} %copy-done.1, s32[1,4096]{1,0:T(1,128)S(1)} %bitcast.18, s32[1,4096]{1,0:T(1,128)S(1)} %bitcast.22, f32[32,535]{1,0:T(8,128)S(1)} %bitcast.17, s32[1,4]{1,0:T(1,128)S(1)} %bitcast.25, ...), custom_call_target="tpu_custom_call" | custom-call | flops 4000000000 | bytes 1048576 | tf_op jit(solution)/shard_map/early/pallas_call | solution.py:491
  11.5 4.0 %all-to-all-done = f32[8,64,128]{2,1,0:T(8,128)S(1)} async-done(((f32[8,64,128]{2,1,0:T(8,128)}), f32[8,64,128]{2,1,0:T(8,128)S(1)}, u32[]{:S(2)}, u32[]{:S(2)}) %all-to-all-start) | async-done | bytes 262176 | tf_op jit(solution)/shard_map/all_to_all | solution.py:509
  15.6 0.0 copy-done.10
  15.6 4.4 %forward.1 = (f32[256,128]{1,0:T(8,128)}, f32[128,4096]{1,0:T(8,128)S(1)}, f32[32,4096]{1,0:T(8,128)S(1)}, bf16[128,256]{1,0:T(8,128)(2,1)S(1)}, f32[8,128]{1,0:T(8,128)S(1)}, /*index=5*/f32[8,8,128]{2,1,0:T(8,128)}) custom-call(s32[1,1]{1,0:T(1,128)} %bitcast.14.count_ref, f32[256,128]{1,0:T(8,128)S(1)} %copy-done.1, ...), custom_call_target="tpu_custom_call", output_to_operand_aliasing={{1}: (6, {}), {2}: (7, {})} | custom-call | flops 4000000000 | bytes 1048576 | tf_op jit(solution)/shard_map/forward/pallas_call | solution.py:491
  20.0 3.3 %all-to-all-start.1 = ((f32[8,8,128]{2,1,0:T(8,128)}), f32[8,8,128]{2,1,0:T(8,128)S(1)}, u32[]{:S(2)}, u32[]{:S(2)}) async-start(f32[8,8,128]{2,1,0:T(8,128)} %get-tuple-element.28), calls=%async_computation.1 | async-start | bytes 65536 | tf_op jit(solution)/shard_map/all_to_all | solution.py:509
  23.3 4.0 %backward.1.grads_ref = f32[160,896]{1,0:T(8,128)S(1)} custom-call(s32[1,1]{1,0:T(1,128)} %bitcast.15.count_ref, f32[128,4096]{1,0:T(8,128)S(1)} %get-tuple-element.29.srct_ref, s32[1,4096]{1,0:T(1,128)S(1)} %bitcast.21, s32[1,4096]{1,0:T(1,128)S(1)} %bitcast.23, s32[4,128]{1,0:T(4,128)S(1)} %copy-done.10, f32[160,128]{1,0:T(8,128)S(1)} %get-tuple-element.25.prep_ref, ...), custom_call_target="tpu_custom_call" | custom-call | flops 4000000000 | bytes 1048576 | tf_op jit(solution)/shard_map/backward/pallas_call | solution.py:491
  27.3 0.8 %all-to-all-done.1.totals_ref = f32[8,8,128]{2,1,0:T(8,128)S(1)} async-done(((f32[8,8,128]{2,1,0:T(8,128)}), f32[8,8,128]{2,1,0:T(8,128)S(1)}, u32[]{:S(2)}, u32[]{:S(2)}) %all-to-all-start.1) | async-done | bytes 32800 | tf_op jit(solution)/shard_map/all_to_all | solution.py:509
  28.1 0.1 combine.1
  28.2 13.7 %all_to_all.20.parts_ref = f32[32,8,128]{2,1,0:T(8,128)S(1)} all-to-all(f32[32,8,128]{2,1,0:T(8,128)S(1)} %combine.1), channel_id=1, replica_groups=mesh['nodes'=8,'queries'=4] {'nodes','queries'}, dimensions={0} | all-to-all | bytes 262144 | tf_op jit(solution)/shard_map/all_to_all | solution.py:509
  41.9 10.1 %all_to_all.21.tiles_ref = f32[32,8,128]{2,1,0:T(8,128)S(1)} all-to-all(f32[32,8,128]{2,1,0:T(8,128)S(1)} %spread.1), channel_id=1, replica_groups=mesh['nodes'=8,'queries'=4] {'nodes','queries'}, dimensions={0} | all-to-all | bytes 262144 | tf_op jit(solution)/shard_map/all_to_all | solution.py:509
  52.1 0.8 %unpack.1 = (f32[32,535]{1,0:T(8,128)}, f32[32,32]{1,0:T(8,128)}, f32[32,64]{1,0:T(8,128)}, f32[32,64]{1,0:T(8,128)}, f32[1,64]{1,0:T(1,128)}, /*index=5*/f32[1,4]{1,0:T(1,128)}) custom-call(f32[32,8,128]{2,1,0:T(8,128)S(1)} %all_to_all.21.tiles_ref, f32[8,8,128]{2,1,0:T(8,128)S(1)} %all-to-all-done.1.totals_ref), custom_call_target="tpu_custom_call" | custom-call | flops 1000000 | bytes 1048576 | tf_op jit(solution)/shard_map/unpack/pallas_call | solution.py:491
  (19 shorter events, 0.1 us)
Async XLA Ops:
  0.6 0.9 %copy-start = (f32[256,128]{1,0:T(8,128)S(1)}, f32[256,128]{1,0:T(8,128)}, u32[]{:S(2)}) copy-start(f32[256,128]{1,0:T(8,128)} %state_ref.5) | copy-start | bytes 393220
  1.5 0.7 %copy-start.9 = (s32[1,8,64]{2,1,0:T(8,128)S(1)}, s32[1,8,64]{2,1,0:T(8,128)}, u32[]{:S(2)}) copy-start(s32[1,8,64]{2,1,0:T(8,128)} %param.20) | copy-start | bytes 6148
  2.2 7.1 %copy-start.1 = (f32[256,128]{1,0:T(8,128)S(1)}, f32[256,128]{1,0:T(8,128)}, u32[]{:S(2)}) copy-start(f32[256,128]{1,0:T(8,128)} %state_ref.5) | copy-start | bytes 393220
  2.2 7.1 %copy-start.2 = (f32[535,32]{0,1:T(8,128)S(1)}, f32[535,32]{0,1:T(8,128)}, u32[]{:S(2)}) copy-start(f32[535,32]{0,1:T(8,128)} %param.25) | copy-start | bytes 205444
  2.2 7.1 %copy-start.3 = (s32[4096]{0:T(1024)S(1)}, s32[4096]{0:T(1024)}, u32[]{:S(2)}) copy-start(s32[4096]{0:T(1024)} %param.16) | copy-start | bytes 49156
  2.2 7.1 %copy-start.5 = (s32[4096]{0:T(1024)S(1)}, s32[4096]{0:T(1024)}, u32[]{:S(2)}) copy-start(s32[4096]{0:T(1024)} %param.18) | copy-start | bytes 49156
  2.2 7.1 %copy-start.6 = (f32[32,32]{1,0:T(8,128)S(1)}, f32[32,32]{1,0:T(8,128)}, u32[]{:S(2)}) copy-start(f32[32,32]{1,0:T(8,128)} %layer_ref.5) | copy-start | bytes 12292
  2.3 7.1 %copy-start.7 = (f32[32,64]{1,0:T(8,128)S(1)}, f32[32,64]{1,0:T(8,128)}, u32[]{:S(2)}) copy-start(f32[32,64]{1,0:T(8,128)} %ment_ref.5) | copy-start | bytes 24580
  2.3 7.1 %copy-start.8 = (f32[32,64]{1,0:T(8,128)S(1)}, f32[32,64]{1,0:T(8,128)}, u32[]{:S(2)}) copy-start(f32[32,64]{1,0:T(8,128)} %mquery_ref.3) | copy-start | bytes 24580
  2.3 7.1 %copy-start.11 = (s32[4]{0:T(128)S(1)}, s32[4]{0:T(128)}, u32[]{:S(2)}) copy-start(s32[4]{0:T(128)} %param.21) | copy-start | bytes 52
  2.3 7.1 %copy-start.12 = (s32[4]{0:T(128)S(1)}, s32[4]{0:T(128)}, u32[]{:S(2)}) copy-start(s32[4]{0:T(128)} %param.22) | copy-start | bytes 52
  2.3 7.1 %copy-start.13 = (s32[4]{0:T(128)S(1)}, s32[4]{0:T(128)}, u32[]{:S(2)}) copy-start(s32[4]{0:T(128)} %param.23) | copy-start | bytes 52
  2.3 7.1 %copy-start.14 = (f32[64]{0:T(128)S(1)}, f32[64]{0:T(128)}, u32[]{:S(2)}) copy-start(f32[64]{0:T(128)} %param.29) | copy-start | bytes 772
  3.5 12.1 %all-to-all-start = ((f32[8,64,128]{2,1,0:T(8,128)}), f32[8,64,128]{2,1,0:T(8,128)S(1)}, u32[]{:S(2)}, u32[]{:S(2)}) async-start(f32[8,64,128]{2,1,0:T(8,128)} %send.1), calls=%async_computation | async-start | bytes 524288 | tf_op jit(solution)/shard_map/all_to_all | solution.py:509
  9.4 6.2 %copy-start.4 = (s32[4096]{0:T(1024)S(1)}, s32[4096]{0:T(1024)}, u32[]{:S(2)}) copy-start(s32[4096]{0:T(1024)} %param.17) | copy-start | bytes 49156
  9.4 6.2 %copy-start.10 = (s32[4,128]{1,0:T(4,128)S(1)}, s32[4,128]{1,0:T(4,128)}, u32[]{:S(2)}) copy-start(s32[4,128]{1,0:T(4,128)} %neg_ref.3) | copy-start | bytes 6148
  20.0 8.1 %all-to-all-start.1 = ((f32[8,8,128]{2,1,0:T(8,128)}), f32[8,8,128]{2,1,0:T(8,128)S(1)}, u32[]{:S(2)}, u32[]{:S(2)}) async-start(f32[8,8,128]{2,1,0:T(8,128)} %get-tuple-element.28), calls=%async_computation.1 | async-start | bytes 65536 | tf_op jit(solution)/shard_map/all_to_all | solution.py:509

commit v3 on v2

--- a/solution.py
+++ b/solution.py
@@ -87,6 +87,22 @@
     return jnp.concatenate([pieces[spot] for spot in RIGHT[terms]], axis=axis)
 
 
+def pick_lanes(table, index_row, otherwise):
+    rows, size = table.shape
+    parts = []
+    for left in range(0, index_row.shape[1], LANES):
+        index = index_row[:, left : left + LANES]
+        low = jnp.broadcast_to(index & (LANES - 1), (rows, LANES))
+        tile = index >> (LANES.bit_length() - 1)
+        found = otherwise[:, left : left + LANES]
+        for spot in range(size // LANES):
+            block = table[:, spot * LANES : (spot + 1) * LANES]
+            taken = jnp.take_along_axis(block, low, axis=1, mode="promise_in_bounds")
+            found = jnp.where(tile == spot, taken, found)
+        parts.append(found)
+    return jnp.concatenate(parts, axis=1)
+
+
 def local_row(entity, ent_local):
     node = lax.axis_index("nodes")
     return jnp.where(entity // ent_local == node, entity % ent_local, -1)
@@ -125,15 +141,20 @@
     return [slice(low, high) for low, high in zip(ends, ends[1:])]
 
 
-def send_kernel(send_ref, state_ref, out_ref):
+def tick_kernel(out_ref):
+    out_ref[...] = jnp.zeros(out_ref.shape, F32)
+
+
+def send_kernel(tick_ref, send_ref, state_ref, out_ref):
     count, bound = send_ref.shape
     ent = state_ref.shape[0]
     pieces = split(state_ref[...], FORWARD, axis=1)
     wanted = send_ref[...].T
     entity = lax.broadcasted_iota(jnp.int32, (bound, ent), 1)
+    hot = [jnp.where(entity == wanted[:, n : n + 1], 1.0, 0.0).astype(BF16) for n in range(count)]
+    rows = join(dot_nn(jnp.concatenate(hot, axis=0), pieces), FORWARD, axis=1)
     for n in range(count):
-        hot = (entity == wanted[:, n : n + 1]).astype(F32).astype(BF16)
-        out_ref[n] = join(dot_nn(hot, pieces), FORWARD, axis=1)
+        out_ref[n] = rows[n * bound : (n + 1) * bound]
 
 
 def early_kernel(
@@ -209,13 +230,24 @@
     q_local, neg = neg_ref.shape
     per_query = neg // LANES
     layout = kept_layout(q_local, ent, neg)
-    recv_bits = split(recv_ref[...].T, FORWARD)
+    recv_t = recv_ref[...].T
+    near = min(256, recv_t.shape[1])
+    recv_bits = split(recv_t[:, near:], FORWARD)
     live = count_ref[...]
     total = jnp.zeros((FORWARD * blocks, ent), F32)
+    def fetch(start):
+        span = slice(start, start + chunk)
+        slot = src_ref[:, span] - ent
+        first = pick_lanes(recv_t[:, :near], slot, local_ref[:, span])
+        return first, dot_nn(recv_bits, one_hot(slot - near, recv_bits.shape[1]))
+
+    coming = fetch(0)
     for start in range(0, edges, chunk):
         span = slice(start, start + chunk)
-        far = one_hot(src_ref[:, span] - ent, recv_bits.shape[1])
-        source = local_ref[:, span] + join(dot_nn(recv_bits, far), FORWARD)
+        remote = coming
+        if start + chunk < edges:
+            coming = fetch(start + chunk)
+        source = remote[0] + join(remote[1], FORWARD)
         srct_ref[:, span] = source
         message = source * jnp.concatenate([relation_ref[:, span]] * q_local, axis=0)
         spot = lax.broadcasted_iota(jnp.int32, (1, chunk), 1) + start
@@ -243,10 +275,8 @@
         new = state_t[rows] + jnp.maximum(mine, 0.0)
         new_parts.append(new)
         own_tail = jnp.where(lane_row == q, tails, -1)
-        hot = one_hot(jnp.concatenate([neg_ref[q : q + 1, :], own_tail], axis=1), ent)
-        picked = join(dot_nn(split(new, FORWARD), hot), FORWARD)
-        picks.append(picked[:, :neg])
-        last = picked[:, neg:]
+        picks.append(pick_lanes(new, neg_ref[q : q + 1, :], jnp.zeros((width, neg), F32)))
+        last = pick_lanes(new, own_tail, jnp.zeros((width, LANES), F32))
         positive = last if positive is None else positive + last
     new_ref[...] = jnp.concatenate(new_parts, axis=0).T
     picked = jnp.concatenate(picks + [positive], axis=1)
@@ -293,14 +323,11 @@
     coef = jnp.where(spot < tail_row, coef, 0.0)
     coef = jnp.where((spot == tail_row) & present, -missing, coef)
     coef_ref[...] = coef * (1.0 / queries_total)
-    tall = totals_ref.shape[1]
-    pair = jnp.where(
-        lax.broadcasted_iota(jnp.int32, (tall, LANES), 1) == 0,
-        fill_rows(owns, tall),
-        fill_rows(weighteds, tall),
-    )
-    down = lax.broadcasted_iota(jnp.int32, (tall, LANES), 0)
-    tile = jnp.where(down == tall - 1, positives, pair)
+    tile = jnp.zeros((1, LANES), F32)
+    for q in range(q_local):
+        tile = jnp.where(lane_row == q, owns[q], tile)
+        tile = jnp.where(lane_row == q_local + q, weighteds[q], tile)
+        tile = jnp.where(lane_row == 2 * q_local + q, positives[:, q : q + 1], tile)
     for n in range(totals_ref.shape[0]):
         totals_ref[n] = tile
 
@@ -369,19 +396,26 @@
     ]
 
     live = count_ref[...]
+
+    def fetch(start):
+        spot = lax.broadcasted_iota(jnp.int32, (1, chunk), 1) + start
+        ends = jnp.where(spot < live, dst_ref[:, start : start + chunk], -2)
+        return ends, dot_nn(sum_bits, one_hot(ends, ent))
+
     total = jnp.zeros((BACKWARD * (blocks + width), rel_rows), F32)
+    coming = fetch(0)
     for start in range(0, edges, chunk):
         span = slice(start, start + chunk)
-        spot = lax.broadcasted_iota(jnp.int32, (1, chunk), 1) + start
-        ends = jnp.where(spot < live, dst_ref[:, span], -2)
+        ends, upstream = coming
+        if start + chunk < edges:
+            coming = fetch(start + chunk)
         source = srct_ref[:, span]
-        upstream = join(dot_nn(sum_bits, one_hot(ends, ent)), BACKWARD)
         tail_terms = jnp.zeros((width, chunk), F32)
         for q in range(q_local):
             rows = slice(q * width, (q + 1) * width)
             hit = (ends == tails[:, q : q + 1]).astype(F32)
             tail_terms = tail_terms + (tail_columns[q] * hit) * source[rows]
-        terms = jnp.concatenate([upstream * source, tail_terms], axis=0)
+        terms = jnp.concatenate([join(upstream, BACKWARD) * source, tail_terms], axis=0)
         total = total + dot_nt(split(terms, BACKWARD), one_hot(rel_ref[:, span], rel_rows))
     gathered = join(total, BACKWARD)
     if rel_lanes > rel_rows:
@@ -415,7 +449,7 @@
             layers = dot_nt(left, right)
             layer_part = layers[:, :width]
             tail_layer = tail_layer + layers[:, width:]
-            vectors = jnp.broadcast_to(prep_ref[:width, q : q + 1], (width, neg))
+            vectors = prep_ref[:width, q : q + 1] + jnp.zeros((width, neg), F32)
             coef_rows = coef_parts[q * per_query : (q + 1) * per_query]
         else:
             span = slice(last, last + LANES)
@@ -425,10 +459,11 @@
         size = span.stop - span.start
         coef = jnp.broadcast_to(jnp.concatenate(coef_rows, axis=1), (width, size))
         right = jnp.concatenate([grad_hidden[:, span], jnp.maximum(hidden[:, span], 0.0)], axis=0)
-        right = stack_right(right, 3, axis=1)
-        entity_part = dot_nt(stack_left(picked[:, span], 3), right)[:, :hid]
-        query_part = dot_nt(stack_left(vectors, 3), right)[:, :hid]
-        score_part = dot_nt(stack_left(coef, 3), right)[:, hid:]
+        left = jnp.concatenate([picked[:, span], vectors, coef], axis=0)
+        products = dot_nt(stack_left(left, 3), stack_right(right, 3, axis=1))
+        entity_part = products[:width, :hid]
+        query_part = products[width : 2 * width, :hid]
+        score_part = products[2 * width :, hid:]
         rest = [layer_part, entity_part, query_part, score_part, spare]
         out_ref[block * width : (block + 1) * width, rel_lanes:] = jnp.concatenate(rest, axis=1)
     seeds.append(tail_seed)
@@ -441,7 +476,7 @@
     scale = totals_ref[lax.axis_index("nodes")] / total
     mixed = grads_ref[q_local * width :, :]
     for q in range(q_local):
-        mixed = mixed + grads_ref[q * width : (q + 1) * width, :] * scale[q : q + 1, 0:1]
+        mixed = mixed + grads_ref[q * width : (q + 1) * width, :] * scale[:, q : q + 1]
     across = mixed.shape[1] // LANES
     tiles = width // SUBLANES * across
     for tile in range(tiles):
@@ -482,8 +517,8 @@
     score_ref[...] = flat[0:1, start : start + hid]
     everyone = jnp.sum(totals_ref[...], axis=0)
     count = loss_ref.shape[1]
-    ratio = as_row(everyone[:count, 1:2] / everyone[:count, 0:1])
-    loss_ref[...] = everyone[-1:, :count] + ratio
+    ratio = everyone[:, count : 2 * count] / everyone[:, :count]
+    loss_ref[...] = everyone[:, 2 * count : 3 * count] + ratio
 
 
 def call(kernel, name, outs, flops, *operands, scratch=(), limit=40 << 20, far=(), alias=None):
@@ -536,15 +571,16 @@
     bound = send_list.shape[2]
     neg = neg_ids.shape[1]
     columns = q_local * neg + LANES
-    chunk = min(1024, edges)
+    chunk = min(512, edges)
     src_row = edge_src.reshape(1, edges)
     dst_row = edge_dst.reshape(1, edges)
     rel_row = edge_rel.reshape(1, edges)
     count = edge_count.reshape(1, 1)
     score_row = score_weight.reshape(1, hid)
     table_t = rel_table.T
+    tick = call(tick_kernel, "tick", [(SUBLANES, LANES)], 10**10)
     outgoing = call(
-        send_kernel, "send", [(nodes, bound, width_all)], 10**9, send_list[0], state_in
+        send_kernel, "send", [(nodes, bound, width_all)], 10**9, tick, send_list[0], state_in
     )
     received = swap(outgoing, "nodes").reshape(nodes * bound, width_all)
     local, relation, prep, marks = call(
@@ -579,7 +615,7 @@
             (width, max(needed, edges)),
             jax.ShapeDtypeStruct((width_all, ent), BF16),
             (pad_to(columns // LANES, SUBLANES), LANES),
-            (nodes, pad_to(q_local + 1, SUBLANES), LANES),
+            (nodes, 1, LANES),
         ],
         4 * 10**9,
         count,

time: 53.2 us -> 51.8 us (0.974)
  local copies, waits for them, and re-layouts: 1.64 us -> 0.95 us
  Pallas kernels: 12.6 us -> 12 us
    unnamed x30 -> x28, local copies, waits for them, and re-layouts: 1.64 us -> 0.95 us
    pallas_call x7 -> x8, Pallas kernels: 12.6 us -> 12 us  [call(): pl.pallas_call(kernel, out_shape=tuple((dims if isinstance(dims, jax.Shap...]
  transfers between devices with their start and end apart: 2 -> 2, of which waited for: 2 -> 2; matrix products, arithmetic and copies ran while one was open for 0% -> 0% of each run, Pallas kernels for 12% -> 11%
where the time goes in v3:
time: 51.8 us; the launch traced here: 51.5 us
  blocking collectives  23.7 us (46%)
  Pallas kernels  12 us (23%)
  starting transfers between devices  8.49 us (16%)
  waiting for transfers between devices  4.89 us (9%)
  between operations  1.49 us (3%)
  local copies, waits for them, and re-layouts  0.95 us (2%)
    all_to_all x2, blocking collectives, swap(): return lax.all_to_all(values, axes, split_axis=0, concat_axis=0, tiled=True)  23.7 us
    pallas_call x8, Pallas kernels, call(): pl.pallas_call(kernel, out_shape=tuple((dims if isinstance(dims, jax.Shap...  12 us
    all_to_all x2, starting transfers between devices, swap(): return lax.all_to_all(values, axes, split_axis=0, concat_axis=0, tiled=True)  8.49 us
    all_to_all x2, waiting for transfers between devices, swap(): return lax.all_to_all(values, axes, split_axis=0, concat_axis=0, tiled=True)  4.89 us
  transfers between devices with their start and end apart: 2, of which 2 were waited for; matrix products, arithmetic and copies ran while one was open for 0% of the time, Pallas kernels for 11%

profile of v3, /device:TPU:0, one launch (start us, length us, event | category | flops | bytes accessed | tf_op | source)
XLA Modules:
  0.0 51.5 jit_solution(519076408875273308)
XLA Ops:
  0.7 0.9 %copy-done = f32[256,128]{1,0:T(8,128)S(1)} copy-done((f32[256,128]{1,0:T(8,128)S(1)}, f32[256,128]{1,0:T(8,128)}, u32[]{:S(2)}) %copy-start) | copy-done | bytes 131096
  1.5 0.0 copy-done.8
  1.5 0.0 copy-start.5
  1.6 0.0 copy-start.6
  1.6 0.0 copy-start.7
  1.6 0.0 copy-start.10
  1.6 0.0 copy-start.11
  1.6 0.0 copy-start.12
  1.6 0.0 copy-start.13
  1.6 1.1 %send.1 = f32[8,64,128]{2,1,0:T(8,128)} custom-call(f32[8,128]{1,0:T(8,128)S(1)} %tick.1.tick_ref, s32[8,64]{1,0:T(8,128)S(1)} %bitcast.24, f32[256,128]{1,0:T(8,128)S(1)} %copy-done), custom_call_target="tpu_custom_call" | custom-call | flops 1000000000 | bytes 1048576 | tf_op jit(solution)/shard_map/send/pallas_call | solution.py:526
  2.7 5.2 %all-to-all-start = ((f32[8,64,128]{2,1,0:T(8,128)}), f32[8,64,128]{2,1,0:T(8,128)S(1)}, u32[]{:S(2)}, u32[]{:S(2)}) async-start(f32[8,64,128]{2,1,0:T(8,128)} %send.1), calls=%async_computation | async-start | bytes 524288 | tf_op jit(solution)/shard_map/all_to_all | solution.py:544
  8.7 0.0 copy-start.3
  8.7 0.0 copy-start.9
  8.7 2.1 %early.1 = (f32[128,4096]{1,0:T(8,128)S(1)}, f32[32,4096]{1,0:T(8,128)S(1)}, f32[160,128]{1,0:T(8,128)S(1)}, s32[8,128]{1,0:T(8,128)S(1)}) custom-call(f32[256,128]{1,0:T(8,128)S(1)} %copy-done, s32[1,4096]{1,0:T(1,128)S(1)} %bitcast.18, s32[1,4096]{1,0:T(1,128)S(1)} %bitcast.22, f32[32,535]{1,0:T(8,128)S(1)} %bitcast.17, s32[1,4]{1,0:T(1,128)S(1)} %bitcast.25, ...), custom_call_target="tpu_custom_call" | custom-call | flops 4000000000 | bytes 1048576 | tf_op jit(solution)/shard_map/early/pallas_call | solution.py:526
  10.8 4.0 %all-to-all-done = f32[8,64,128]{2,1,0:T(8,128)S(1)} async-done(((f32[8,64,128]{2,1,0:T(8,128)}), f32[8,64,128]{2,1,0:T(8,128)S(1)}, u32[]{:S(2)}, u32[]{:S(2)}) %all-to-all-start) | async-done | bytes 262176 | tf_op jit(solution)/shard_map/all_to_all | solution.py:544
  14.9 0.0 copy-done.3
  14.9 4.1 %forward.1 = (f32[256,128]{1,0:T(8,128)}, f32[128,4096]{1,0:T(8,128)S(1)}, f32[32,4096]{1,0:T(8,128)S(1)}, bf16[128,256]{1,0:T(8,128)(2,1)S(1)}, f32[8,128]{1,0:T(8,128)S(1)}, /*index=5*/f32[8,1,128]{2,1,0:T(1,128)}) custom-call(s32[1,1]{1,0:T(1,128)} %bitcast.14.count_ref, f32[256,128]{1,0:T(8,128)S(1)} %copy-done, ...), custom_call_target="tpu_custom_call", output_to_operand_aliasing={{1}: (6, {}), {2}: (7, {})} | custom-call | flops 4000000000 | bytes 1048576 | tf_op jit(solution)/shard_map/forward/pallas_call | solution.py:526
  19.0 3.3 %all-to-all-start.1 = ((f32[8,1,128]{2,1,0:T(1,128)}), f32[8,1,128]{2,1,0:T(1,128)S(1)}, u32[]{:S(2)}, u32[]{:S(2)}) async-start(f32[8,1,128]{2,1,0:T(1,128)} %get-tuple-element.28), calls=%async_computation.1 | async-start | bytes 8192 | tf_op jit(solution)/shard_map/all_to_all | solution.py:544
  22.3 3.7 %backward.1.grads_ref = f32[160,896]{1,0:T(8,128)S(1)} custom-call(s32[1,1]{1,0:T(1,128)} %bitcast.15.count_ref, f32[128,4096]{1,0:T(8,128)S(1)} %get-tuple-element.29.srct_ref, s32[1,4096]{1,0:T(1,128)S(1)} %bitcast.21, s32[1,4096]{1,0:T(1,128)S(1)} %bitcast.23, s32[4,128]{1,0:T(4,128)S(1)} %copy-done.9, f32[160,128]{1,0:T(8,128)S(1)} %get-tuple-element.25.prep_ref, ...), custom_call_target="tpu_custom_call" | custom-call | flops 4000000000 | bytes 1048576 | tf_op jit(solution)/shard_map/backward/pallas_call | solution.py:526
  26.0 0.8 %all-to-all-done.1.totals_ref = f32[8,1,128]{2,1,0:T(1,128)S(1)} async-done(((f32[8,1,128]{2,1,0:T(1,128)}), f32[8,1,128]{2,1,0:T(1,128)S(1)}, u32[]{:S(2)}, u32[]{:S(2)}) %all-to-all-start.1) | async-done | bytes 4128 | tf_op jit(solution)/shard_map/all_to_all | solution.py:544
  26.8 0.1 combine.1
  27.0 13.6 %all_to_all.20.parts_ref = f32[32,8,128]{2,1,0:T(8,128)S(1)} all-to-all(f32[32,8,128]{2,1,0:T(8,128)S(1)} %combine.1), channel_id=1, replica_groups=mesh['nodes'=8,'queries'=4] {'nodes','queries'}, dimensions={0} | all-to-all | bytes 262144 | tf_op jit(solution)/shard_map/all_to_all | solution.py:544
  40.6 10.1 %all_to_all.21.tiles_ref = f32[32,8,128]{2,1,0:T(8,128)S(1)} all-to-all(f32[32,8,128]{2,1,0:T(8,128)S(1)} %spread.1), channel_id=1, replica_groups=mesh['nodes'=8,'queries'=4] {'nodes','queries'}, dimensions={0} | all-to-all | bytes 262144 | tf_op jit(solution)/shard_map/all_to_all | solution.py:544
  50.7 0.8 %unpack.1 = (f32[32,535]{1,0:T(8,128)}, f32[32,32]{1,0:T(8,128)}, f32[32,64]{1,0:T(8,128)}, f32[32,64]{1,0:T(8,128)}, f32[1,64]{1,0:T(1,128)}, /*index=5*/f32[1,4]{1,0:T(1,128)}) custom-call(f32[32,8,128]{2,1,0:T(8,128)S(1)} %all_to_all.21.tiles_ref, f32[8,1,128]{2,1,0:T(1,128)S(1)} %all-to-all-done.1.totals_ref), custom_call_target="tpu_custom_call" | custom-call | flops 1000000 | bytes 1048576 | tf_op jit(solution)/shard_map/unpack/pallas_call | solution.py:526
  (18 shorter events, 0.1 us)
Async XLA Ops:
  0.6 0.9 %copy-start = (f32[256,128]{1,0:T(8,128)S(1)}, f32[256,128]{1,0:T(8,128)}, u32[]{:S(2)}) copy-start(f32[256,128]{1,0:T(8,128)} %state_ref.5) | copy-start | bytes 393220
  0.6 0.9 %copy-start.8 = (s32[1,8,64]{2,1,0:T(8,128)S(1)}, s32[1,8,64]{2,1,0:T(8,128)}, u32[]{:S(2)}) copy-start(s32[1,8,64]{2,1,0:T(8,128)} %param.20) | copy-start | bytes 6148
  1.5 7.0 %copy-start.1 = (f32[535,32]{0,1:T(8,128)S(1)}, f32[535,32]{0,1:T(8,128)}, u32[]{:S(2)}) copy-start(f32[535,32]{0,1:T(8,128)} %param.25) | copy-start | bytes 205444
  1.5 7.0 %copy-start.2 = (s32[4096]{0:T(1024)S(1)}, s32[4096]{0:T(1024)}, u32[]{:S(2)}) copy-start(s32[4096]{0:T(1024)} %param.16) | copy-start | bytes 49156
  1.5 7.1 %copy-start.4 = (s32[4096]{0:T(1024)S(1)}, s32[4096]{0:T(1024)}, u32[]{:S(2)}) copy-start(s32[4096]{0:T(1024)} %param.18) | copy-start | bytes 49156
  1.5 7.1 %copy-start.5 = (f32[32,32]{1,0:T(8,128)S(1)}, f32[32,32]{1,0:T(8,128)}, u32[]{:S(2)}) copy-start(f32[32,32]{1,0:T(8,128)} %layer_ref.5) | copy-start | bytes 12292
  1.6 7.1 %copy-start.6 = (f32[32,64]{1,0:T(8,128)S(1)}, f32[32,64]{1,0:T(8,128)}, u32[]{:S(2)}) copy-start(f32[32,64]{1,0:T(8,128)} %ment_ref.5) | copy-start | bytes 24580
  1.6 7.1 %copy-start.7 = (f32[32,64]{1,0:T(8,128)S(1)}, f32[32,64]{1,0:T(8,128)}, u32[]{:S(2)}) copy-start(f32[32,64]{1,0:T(8,128)} %mquery_ref.3) | copy-start | bytes 24580
  1.6 7.1 %copy-start.10 = (s32[4]{0:T(128)S(1)}, s32[4]{0:T(128)}, u32[]{:S(2)}) copy-start(s32[4]{0:T(128)} %param.21) | copy-start | bytes 52
  1.6 7.1 %copy-start.11 = (s32[4]{0:T(128)S(1)}, s32[4]{0:T(128)}, u32[]{:S(2)}) copy-start(s32[4]{0:T(128)} %param.22) | copy-start | bytes 52
  1.6 7.0 %copy-start.12 = (s32[4]{0:T(128)S(1)}, s32[4]{0:T(128)}, u32[]{:S(2)}) copy-start(s32[4]{0:T(128)} %param.23) | copy-start | bytes 52
  1.6 7.0 %copy-start.13 = (f32[64]{0:T(128)S(1)}, f32[64]{0:T(128)}, u32[]{:S(2)}) copy-start(f32[64]{0:T(128)} %param.29) | copy-start | bytes 772
  2.7 12.1 %all-to-all-start = ((f32[8,64,128]{2,1,0:T(8,128)}), f32[8,64,128]{2,1,0:T(8,128)S(1)}, u32[]{:S(2)}, u32[]{:S(2)}) async-start(f32[8,64,128]{2,1,0:T(8,128)} %send.1), calls=%async_computation | async-start | bytes 524288 | tf_op jit(solution)/shard_map/all_to_all | solution.py:544
  8.7 6.2 %copy-start.3 = (s32[4096]{0:T(1024)S(1)}, s32[4096]{0:T(1024)}, u32[]{:S(2)}) copy-start(s32[4096]{0:T(1024)} %param.17) | copy-start | bytes 49156
  8.7 6.2 %copy-start.9 = (s32[4,128]{1,0:T(4,128)S(1)}, s32[4,128]{1,0:T(4,128)}, u32[]{:S(2)}) copy-start(s32[4,128]{1,0:T(4,128)} %neg_ref.3) | copy-start | bytes 6148
  19.0 7.8 %all-to-all-start.1 = ((f32[8,1,128]{2,1,0:T(1,128)}), f32[8,1,128]{2,1,0:T(1,128)S(1)}, u32[]{:S(2)}, u32[]{:S(2)}) async-start(f32[8,1,128]{2,1,0:T(1,128)} %get-tuple-element.28), calls=%async_computation.1 | async-start | bytes 8192 | tf_op jit(solution)/shard_map/all_to_all | solution.py:544

commit v4 on v3

--- a/solution.py
+++ b/solution.py
@@ -15,7 +15,6 @@
 SUBLANES = 8
 FORWARD = 3
 BACKWARD = 2
-SEND_LIMIT = 64 << 20
 
 
 def pad_to(count, unit):
@@ -137,7 +136,9 @@
 
 def kept_layout(q_local, ent, neg, parts=2):
     columns = q_local * neg + LANES
-    ends = [0, q_local * ent] + [q_local * ent + (part + 1) * columns for part in range(1 + parts)]
+    ends = [0]
+    for size in [q_local * ent] + [columns] * (1 + parts) + [q_local * ent]:
+        ends.append(ends[-1] + size)
     return [slice(low, high) for low, high in zip(ends, ends[1:])]
 
 
@@ -216,14 +217,13 @@
     marks_ref,
     layer_ref,
     ment_ref,
-    new_ref,
     srct_ref,
     kept_ref,
     gate_ref,
     coef_ref,
     totals_ref,
 ):
-    chunk, queries_total = sizes
+    (chunk,) = sizes
     ent, blocks = state_ref.shape
     edges = src_ref.shape[1]
     width, hid = ment_ref.shape
@@ -278,7 +278,7 @@
         picks.append(pick_lanes(new, neg_ref[q : q + 1, :], jnp.zeros((width, neg), F32)))
         last = pick_lanes(new, own_tail, jnp.zeros((width, LANES), F32))
         positive = last if positive is None else positive + last
-    new_ref[...] = jnp.concatenate(new_parts, axis=0).T
+    kept_ref[:, layout[-1]] = jnp.concatenate(new_parts, axis=1)
     picked = jnp.concatenate(picks + [positive], axis=1)
     kept_ref[:, layout[1]] = picked
     plain = dot_nn(stack_left(ment_ref[...].T, 6), stack_right(picked, 6))
@@ -295,21 +295,16 @@
             kept_ref[:, left : left + LANES] = hidden[part * width : (part + 1) * width]
         weighted = jnp.maximum(hidden, 0.0) * prep_ref[width + hid :, :]
         rows.append(jnp.sum(weighted, axis=0, keepdims=True))
-    height = coef_ref.shape[0]
+    height = coef_ref.shape[0] // 2
     scores = fill_rows(rows, height)
     weights = jnp.exp(adversarial * scores)
-    decay = jnp.exp(-jnp.abs(scores))
-    near = jnp.log1p(decay)
-    softplus = jnp.maximum(scores, 0.0) + near
-    flipped = jnp.maximum(-scores, 0.0) + near
-    share = 1.0 / (1.0 + decay)
-    sigmoid = jnp.where(scores >= 0.0, share, decay * share)
-    missing = jnp.where(scores >= 0.0, decay * share, share)
+    near_zero = jnp.log1p(jnp.exp(-jnp.abs(scores)))
+    softplus = jnp.maximum(scores, 0.0) + near_zero
+    flipped = jnp.maximum(-scores, 0.0) + near_zero
     row_total = jnp.sum(weights, axis=1, keepdims=True)
     row_weighted = jnp.sum(weights * softplus, axis=1, keepdims=True)
-    present = (tails >= 0) & (lane_row < q_local)
     tail_row = len(rows) - 1
-    positives = jnp.where(present, flipped[tail_row : tail_row + 1], 0.0)
+    positives = jnp.where(tails >= 0, flipped[tail_row : tail_row + 1], 0.0)
     owns, weighteds, row_owns = [], [], []
     for q in range(q_local):
         mine = slice(q * per_query, (q + 1) * per_query)
@@ -317,12 +312,8 @@
         owns.append(own)
         row_owns.extend([own] * per_query)
         weighteds.append(jnp.sum(row_weighted[mine], axis=0, keepdims=True))
-    row_own = fill_rows(row_owns, height)
-    coef = weights * sigmoid / jnp.where(row_own > 0.0, row_own, 1.0)
-    spot = lax.broadcasted_iota(jnp.int32, (height, LANES), 0)
-    coef = jnp.where(spot < tail_row, coef, 0.0)
-    coef = jnp.where((spot == tail_row) & present, -missing, coef)
-    coef_ref[...] = coef * (1.0 / queries_total)
+    coef_ref[:height, :] = scores
+    coef_ref[height:, :] = jnp.broadcast_to(fill_rows(row_owns, height), (height, LANES))
     tile = jnp.zeros((1, LANES), F32)
     for q in range(q_local):
         tile = jnp.where(lane_row == q, owns[q], tile)
@@ -348,15 +339,23 @@
     gate_ref,
     coef_ref,
     out_ref,
+    new_hbm,
+    new_ref,
+    sems,
 ):
-    chunk, relations = sizes
+    chunk, relations, queries_total = sizes
     width, hid = ment_ref.shape
     blocks, ent = gate_ref.shape
     q_local, neg = neg_ref.shape
     edges = dst_ref.shape[1]
     layout = kept_layout(q_local, ent, neg)
+    first = layout[-1].start
+    new_parts = [kept_ref[:, first + q * ent : first + (q + 1) * ent] for q in range(q_local)]
+    new_ref[...] = jnp.concatenate(new_parts, axis=0).T
+    new_copy = pltpu.make_async_copy(new_ref, new_hbm, sems.at[0])
+    new_copy.start()
     picked = kept_ref[:, layout[1]]
-    hidden = jnp.concatenate([kept_ref[:, spot] for spot in layout[2:]], axis=0)
+    hidden = jnp.concatenate([kept_ref[:, spot] for spot in layout[2:-1]], axis=0)
     per_query = neg // LANES
     rel_lanes = pad_to(relations, LANES)
     rel_rows = pad_to(relations, 16)
@@ -365,10 +364,22 @@
     qrels = marks_ref[2:3, :]
     entity_row = lax.broadcasted_iota(jnp.int32, (1, ent), 1)
     rel_row = lax.broadcasted_iota(jnp.int32, (1, rel_lanes), 1)
+    height = coef_ref.shape[0] // 2
+    scores, row_own = coef_ref[:height, :], coef_ref[height:, :]
+    decay = jnp.exp(-jnp.abs(scores))
+    share = 1.0 / (1.0 + decay)
+    sigmoid = jnp.where(scores >= 0.0, share, decay * share)
+    missing = jnp.where(scores >= 0.0, decay * share, share)
+    weights = jnp.exp(adversarial * scores)
+    coefs = weights * sigmoid / jnp.where(row_own > 0.0, row_own, 1.0)
+    spot = lax.broadcasted_iota(jnp.int32, (height, LANES), 0)
+    tail_row = hidden.shape[1] // LANES - 1
+    coefs = jnp.where(spot < tail_row, coefs, 0.0)
+    coefs = jnp.where((spot == tail_row) & (tails >= 0), -missing, coefs) * (1.0 / queries_total)
     grad_parts, coef_parts = [], []
     for block in range(hidden.shape[1] // LANES):
         span = slice(block * LANES, (block + 1) * LANES)
-        coef = coef_ref[block : block + 1, :]
+        coef = coefs[block : block + 1, :]
         coef_parts.append(coef)
         grad_parts.append(
             jnp.where(hidden[:, span] > 0.0, coef * prep_ref[width + hid :, :], 0.0)
@@ -468,6 +479,7 @@
         out_ref[block * width : (block + 1) * width, rel_lanes:] = jnp.concatenate(rest, axis=1)
     seeds.append(tail_seed)
     out_ref[:, :rel_lanes] = gathered + jnp.concatenate(seeds, axis=0)
+    new_copy.wait()
 
 
 def combine_kernel(sizes, totals_ref, grads_ref, sent_ref):
@@ -521,19 +533,19 @@
     loss_ref[...] = everyone[:, 2 * count : 3 * count] + ratio
 
 
-def call(kernel, name, outs, flops, *operands, scratch=(), limit=40 << 20, far=(), alias=None):
-    spaces = [pltpu.HBM if spot in far else pltpu.VMEM for spot in range(len(operands))]
+def call(kernel, name, outs, flops, *operands, scratch=(), far_out=(), alias=None):
+    spaces = [pl.ANY if spot in far_out else pltpu.VMEM for spot in range(len(outs))]
     found = pl.pallas_call(
         kernel,
         out_shape=tuple(
             dims if isinstance(dims, jax.ShapeDtypeStruct) else jax.ShapeDtypeStruct(dims, F32)
             for dims in outs
         ),
-        in_specs=[pl.BlockSpec(memory_space=space) for space in spaces],
-        out_specs=tuple(pl.BlockSpec(memory_space=pltpu.VMEM) for _ in outs),
+        in_specs=[pl.BlockSpec(memory_space=pltpu.VMEM) for _ in operands],
+        out_specs=tuple(pl.BlockSpec(memory_space=space) for space in spaces),
         scratch_shapes=scratch,
         input_output_aliases=alias or {},
-        compiler_params=pltpu.CompilerParams(vmem_limit_bytes=limit),
+        compiler_params=pltpu.CompilerParams(vmem_limit_bytes=40 << 20),
         cost_estimate=pl.CostEstimate(flops=flops, bytes_accessed=1 << 20, transcendentals=0),
         name=name,
     )(*operands)
@@ -606,15 +618,14 @@
         score_row,
     )
     needed = kept_layout(q_local, ent, neg)[-1].stop
-    new_state, source_t, kept, gate, coef, totals = call(
-        functools.partial(forward_kernel, (chunk, q_local * queries)),
+    source_t, kept, gate, coef, totals = call(
+        functools.partial(forward_kernel, (chunk,)),
         "forward",
         [
-            (ent, width_all),
             (width_all, edges),
             (width, max(needed, edges)),
             jax.ShapeDtypeStruct((width_all, ent), BF16),
-            (pad_to(columns // LANES, SUBLANES), LANES),
+            (2 * pad_to(columns // LANES, SUBLANES), LANES),
             (nodes, 1, LANES),
         ],
         4 * 10**9,
@@ -630,16 +641,16 @@
         marks,
         layer_weight,
         mlp_entity,
-        alias={6: 1, 7: 2} if needed <= edges else {6: 1},
+        alias={6: 0, 7: 1} if needed <= edges else {6: 0},
     )
     all_totals = swap(totals, "nodes")
     rel_lanes = pad_to(relations, LANES)
     lanes = rel_lanes + pad_to(width + 3 * hid, LANES)
     across = lanes // LANES
-    grads = call(
-        functools.partial(backward_kernel, (chunk, relations)),
+    grads, new_state = call(
+        functools.partial(backward_kernel, (chunk, relations, q_local * queries)),
         "backward",
-        [((q_local + 1) * width, lanes)],
+        [((q_local + 1) * width, lanes), (ent, width_all)],
         4 * 10**9,
         count,
         source_t,
@@ -654,6 +665,8 @@
         kept,
         gate,
         coef,
+        scratch=[pltpu.VMEM((ent, width_all), F32), pltpu.SemaphoreType.DMA((1,))],
+        far_out=(1,),
     )
     tiles = width // SUBLANES * across
     wide = nodes * queries

time: 51.8 us -> 51.7 us (level)
  no operation moved by 1% of the time
where the time goes in v4:
time: 51.7 us; the launch traced here: 51.4 us
  blocking collectives  23.8 us (46%)
  Pallas kernels  11.8 us (23%)
  starting transfers between devices  8.49 us (16%)
  waiting for transfers between devices  4.87 us (9%)
  between operations  1.49 us (3%)
  local copies, waits for them, and re-layouts  0.95 us (2%)
    all_to_all x2, blocking collectives, swap(): return lax.all_to_all(values, axes, split_axis=0, concat_axis=0, tiled=True)  23.8 us
    pallas_call x8, Pallas kernels, call(): pl.pallas_call(kernel, out_shape=tuple((dims if isinstance(dims, jax.Shap...  11.8 us
    all_to_all x2, starting transfers between devices, swap(): return lax.all_to_all(values, axes, split_axis=0, concat_axis=0, tiled=True)  8.49 us
    all_to_all x2, waiting for transfers between devices, swap(): return lax.all_to_all(values, axes, split_axis=0, concat_axis=0, tiled=True)  4.87 us
  transfers between devices with their start and end apart: 2, of which 2 were waited for; matrix products, arithmetic and copies ran while one was open for 0% of the time, Pallas kernels for 11%

profile of v4, /device:TPU:0, one launch (start us, length us, event | category | flops | bytes accessed | tf_op | source)
XLA Modules:
  0.0 51.4 jit_solution(17184993950263208260)
XLA Ops:
  0.6 0.0 copy-start
  0.7 0.9 %copy-done = f32[256,128]{1,0:T(8,128)S(1)} copy-done((f32[256,128]{1,0:T(8,128)S(1)}, f32[256,128]{1,0:T(8,128)}, u32[]{:S(2)}) %copy-start) | copy-done | bytes 131096
  1.5 0.0 copy-done.8
  1.5 0.0 copy-start.5
  1.6 0.0 copy-start.6
  1.6 0.0 copy-start.7
  1.6 0.0 copy-start.10
  1.6 0.0 copy-start.11
  1.6 0.0 copy-start.12
  1.6 0.0 copy-start.13
  1.6 1.1 %send.1 = f32[8,64,128]{2,1,0:T(8,128)} custom-call(f32[8,128]{1,0:T(8,128)S(1)} %tick.1.tick_ref, s32[8,64]{1,0:T(8,128)S(1)} %bitcast.24, f32[256,128]{1,0:T(8,128)S(1)} %copy-done), custom_call_target="tpu_custom_call" | custom-call | flops 1000000000 | bytes 1048576 | tf_op jit(solution)/shard_map/send/pallas_call | solution.py:538
  2.7 5.2 %all-to-all-start = ((f32[8,64,128]{2,1,0:T(8,128)}), f32[8,64,128]{2,1,0:T(8,128)S(1)}, u32[]{:S(2)}, u32[]{:S(2)}) async-start(f32[8,64,128]{2,1,0:T(8,128)} %send.1), calls=%async_computation | async-start | bytes 524288 | tf_op jit(solution)/shard_map/all_to_all | solution.py:556
  8.7 0.0 copy-start.3
  8.7 0.0 copy-start.9
  8.7 2.1 %early.1 = (f32[128,4096]{1,0:T(8,128)S(1)}, f32[32,4096]{1,0:T(8,128)S(1)}, f32[160,128]{1,0:T(8,128)S(1)}, s32[8,128]{1,0:T(8,128)S(1)}) custom-call(f32[256,128]{1,0:T(8,128)S(1)} %copy-done, s32[1,4096]{1,0:T(1,128)S(1)} %bitcast.18, s32[1,4096]{1,0:T(1,128)S(1)} %bitcast.22, f32[32,535]{1,0:T(8,128)S(1)} %bitcast.17, s32[1,4]{1,0:T(1,128)S(1)} %bitcast.25, ...), custom_call_target="tpu_custom_call" | custom-call | flops 4000000000 | bytes 1048576 | tf_op jit(solution)/shard_map/early/pallas_call | solution.py:538
  10.8 4.1 %all-to-all-done = f32[8,64,128]{2,1,0:T(8,128)S(1)} async-done(((f32[8,64,128]{2,1,0:T(8,128)}), f32[8,64,128]{2,1,0:T(8,128)S(1)}, u32[]{:S(2)}, u32[]{:S(2)}) %all-to-all-start) | async-done | bytes 262176 | tf_op jit(solution)/shard_map/all_to_all | solution.py:556
  14.9 4.0 %forward.1 = (f32[128,4096]{1,0:T(8,128)S(1)}, f32[32,4096]{1,0:T(8,128)S(1)}, bf16[128,256]{1,0:T(8,128)(2,1)S(1)}, f32[16,128]{1,0:T(8,128)S(1)}, f32[8,1,128]{2,1,0:T(1,128)}) custom-call(s32[1,1]{1,0:T(1,128)} %bitcast.14.count_ref, f32[256,128]{1,0:T(8,128)S(1)} %copy-done, ...), custom_call_target="tpu_custom_call", output_to_operand_aliasing={{0}: (6, {}), {1}: (7, {})} | custom-call | flops 4000000000 | bytes 1048576 | tf_op jit(solution)/shard_map/forward/pallas_call | solution.py:538
  18.8 3.3 %all-to-all-start.1 = ((f32[8,1,128]{2,1,0:T(1,128)}), f32[8,1,128]{2,1,0:T(1,128)S(1)}, u32[]{:S(2)}, u32[]{:S(2)}) async-start(f32[8,1,128]{2,1,0:T(1,128)} %get-tuple-element.33), calls=%async_computation.1 | async-start | bytes 8192 | tf_op jit(solution)/shard_map/all_to_all | solution.py:556
  22.1 3.7 %backward.1 = (f32[160,896]{1,0:T(8,128)S(1)}, f32[256,128]{1,0:T(8,128)}) custom-call(s32[1,1]{1,0:T(1,128)} %bitcast.15.count_ref, f32[128,4096]{1,0:T(8,128)S(1)} %get-tuple-element.28.srct_ref, s32[1,4096]{1,0:T(1,128)S(1)} %bitcast.21, s32[1,4096]{1,0:T(1,128)S(1)} %bitcast.23, s32[4,128]{1,0:T(4,128)S(1)} %copy-done.9, ...), custom_call_target="tpu_custom_call" | custom-call | flops 4000000000 | bytes 1048576 | tf_op jit(solution)/shard_map/backward/pallas_call | solution.py:538
  25.8 0.8 %all-to-all-done.1.totals_ref = f32[8,1,128]{2,1,0:T(1,128)S(1)} async-done(((f32[8,1,128]{2,1,0:T(1,128)}), f32[8,1,128]{2,1,0:T(1,128)S(1)}, u32[]{:S(2)}, u32[]{:S(2)}) %all-to-all-start.1) | async-done | bytes 4128 | tf_op jit(solution)/shard_map/all_to_all | solution.py:556
  26.7 0.1 combine.1
  26.8 13.7 %all_to_all.20.parts_ref = f32[32,8,128]{2,1,0:T(8,128)S(1)} all-to-all(f32[32,8,128]{2,1,0:T(8,128)S(1)} %combine.1), channel_id=1, replica_groups=mesh['nodes'=8,'queries'=4] {'nodes','queries'}, dimensions={0} | all-to-all | bytes 262144 | tf_op jit(solution)/shard_map/all_to_all | solution.py:556
  40.5 10.1 %all_to_all.21.tiles_ref = f32[32,8,128]{2,1,0:T(8,128)S(1)} all-to-all(f32[32,8,128]{2,1,0:T(8,128)S(1)} %spread.1), channel_id=1, replica_groups=mesh['nodes'=8,'queries'=4] {'nodes','queries'}, dimensions={0} | all-to-all | bytes 262144 | tf_op jit(solution)/shard_map/all_to_all | solution.py:556
  50.6 0.8 %unpack.1 = (f32[32,535]{1,0:T(8,128)}, f32[32,32]{1,0:T(8,128)}, f32[32,64]{1,0:T(8,128)}, f32[32,64]{1,0:T(8,128)}, f32[1,64]{1,0:T(1,128)}, /*index=5*/f32[1,4]{1,0:T(1,128)}) custom-call(f32[32,8,128]{2,1,0:T(8,128)S(1)} %all_to_all.21.tiles_ref, f32[8,1,128]{2,1,0:T(1,128)S(1)} %all-to-all-done.1.totals_ref), custom_call_target="tpu_custom_call" | custom-call | flops 1000000 | bytes 1048576 | tf_op jit(solution)/shard_map/unpack/pallas_call | solution.py:538
  (18 shorter events, 0.1 us)
Async XLA Ops:
  0.6 0.9 %copy-start = (f32[256,128]{1,0:T(8,128)S(1)}, f32[256,128]{1,0:T(8,128)}, u32[]{:S(2)}) copy-start(f32[256,128]{1,0:T(8,128)} %state_ref.5) | copy-start | bytes 393220
  0.6 0.9 %copy-start.8 = (s32[1,8,64]{2,1,0:T(8,128)S(1)}, s32[1,8,64]{2,1,0:T(8,128)}, u32[]{:S(2)}) copy-start(s32[1,8,64]{2,1,0:T(8,128)} %param.20) | copy-start | bytes 6148
  1.5 7.0 %copy-start.1 = (f32[535,32]{0,1:T(8,128)S(1)}, f32[535,32]{0,1:T(8,128)}, u32[]{:S(2)}) copy-start(f32[535,32]{0,1:T(8,128)} %param.25) | copy-start | bytes 205444
  1.5 7.0 %copy-start.2 = (s32[4096]{0:T(1024)S(1)}, s32[4096]{0:T(1024)}, u32[]{:S(2)}) copy-start(s32[4096]{0:T(1024)} %param.16) | copy-start | bytes 49156
  1.5 7.0 %copy-start.4 = (s32[4096]{0:T(1024)S(1)}, s32[4096]{0:T(1024)}, u32[]{:S(2)}) copy-start(s32[4096]{0:T(1024)} %param.18) | copy-start | bytes 49156
  1.5 7.1 %copy-start.5 = (f32[32,32]{1,0:T(8,128)S(1)}, f32[32,32]{1,0:T(8,128)}, u32[]{:S(2)}) copy-start(f32[32,32]{1,0:T(8,128)} %layer_ref.5) | copy-start | bytes 12292
  1.6 7.1 %copy-start.6 = (f32[32,64]{1,0:T(8,128)S(1)}, f32[32,64]{1,0:T(8,128)}, u32[]{:S(2)}) copy-start(f32[32,64]{1,0:T(8,128)} %ment_ref.5) | copy-start | bytes 24580
  1.6 7.1 %copy-start.7 = (f32[32,64]{1,0:T(8,128)S(1)}, f32[32,64]{1,0:T(8,128)}, u32[]{:S(2)}) copy-start(f32[32,64]{1,0:T(8,128)} %mquery_ref.3) | copy-start | bytes 24580
  1.6 7.0 %copy-start.10 = (s32[4]{0:T(128)S(1)}, s32[4]{0:T(128)}, u32[]{:S(2)}) copy-start(s32[4]{0:T(128)} %param.21) | copy-start | bytes 52
  1.6 7.0 %copy-start.11 = (s32[4]{0:T(128)S(1)}, s32[4]{0:T(128)}, u32[]{:S(2)}) copy-start(s32[4]{0:T(128)} %param.22) | copy-start | bytes 52
  1.6 7.0 %copy-start.12 = (s32[4]{0:T(128)S(1)}, s32[4]{0:T(128)}, u32[]{:S(2)}) copy-start(s32[4]{0:T(128)} %param.23) | copy-start | bytes 52
  1.6 7.0 %copy-start.13 = (f32[64]{0:T(128)S(1)}, f32[64]{0:T(128)}, u32[]{:S(2)}) copy-start(f32[64]{0:T(128)} %param.29) | copy-start | bytes 772
  2.7 12.1 %all-to-all-start = ((f32[8,64,128]{2,1,0:T(8,128)}), f32[8,64,128]{2,1,0:T(8,128)S(1)}, u32[]{:S(2)}, u32[]{:S(2)}) async-start(f32[8,64,128]{2,1,0:T(8,128)} %send.1), calls=%async_computation | async-start | bytes 524288 | tf_op jit(solution)/shard_map/all_to_all | solution.py:556
  8.7 6.2 %copy-start.3 = (s32[4096]{0:T(1024)S(1)}, s32[4096]{0:T(1024)}, u32[]{:S(2)}) copy-start(s32[4096]{0:T(1024)} %param.17) | copy-start | bytes 49156
  8.7 6.2 %copy-start.9 = (s32[4,128]{1,0:T(4,128)S(1)}, s32[4,128]{1,0:T(4,128)}, u32[]{:S(2)}) copy-start(s32[4,128]{1,0:T(4,128)} %neg_ref.3) | copy-start | bytes 6148
  18.8 7.8 %all-to-all-start.1 = ((f32[8,1,128]{2,1,0:T(1,128)}), f32[8,1,128]{2,1,0:T(1,128)S(1)}, u32[]{:S(2)}, u32[]{:S(2)}) async-start(f32[8,1,128]{2,1,0:T(1,128)} %get-tuple-element.33), calls=%async_computation.1 | async-start | bytes 8192 | tf_op jit(solution)/shard_map/all_to_all | solution.py:556

commit v5 on v4

--- a/solution.py
+++ b/solution.py
@@ -146,14 +146,20 @@
     out_ref[...] = jnp.zeros(out_ref.shape, F32)
 
 
-def send_kernel(tick_ref, send_ref, state_ref, out_ref):
+def wanted_kernel(tick_ref, send_ref, hot_ref):
     count, bound = send_ref.shape
-    ent = state_ref.shape[0]
-    pieces = split(state_ref[...], FORWARD, axis=1)
+    ent = hot_ref.shape[1]
     wanted = send_ref[...].T
     entity = lax.broadcasted_iota(jnp.int32, (bound, ent), 1)
-    hot = [jnp.where(entity == wanted[:, n : n + 1], 1.0, 0.0).astype(BF16) for n in range(count)]
-    rows = join(dot_nn(jnp.concatenate(hot, axis=0), pieces), FORWARD, axis=1)
+    for n in range(count):
+        same = entity == wanted[:, n : n + 1]
+        hot_ref[n * bound : (n + 1) * bound, :] = jnp.where(same, 1.0, 0.0).astype(BF16)
+
+
+def send_kernel(hot_ref, state_ref, out_ref):
+    count, bound = out_ref.shape[:2]
+    pieces = split(state_ref[...], FORWARD, axis=1)
+    rows = join(dot_nn(hot_ref[...], pieces), FORWARD, axis=1)
     for n in range(count):
         out_ref[n] = rows[n * bound : (n + 1) * bound]
 
@@ -546,7 +552,7 @@
         scratch_shapes=scratch,
         input_output_aliases=alias or {},
         compiler_params=pltpu.CompilerParams(vmem_limit_bytes=40 << 20),
-        cost_estimate=pl.CostEstimate(flops=flops, bytes_accessed=1 << 20, transcendentals=0),
+        cost_estimate=pl.CostEstimate(flops=flops, bytes_accessed=min(flops, 1 << 20), transcendentals=0),
         name=name,
     )(*operands)
     return found[0] if len(outs) == 1 else found
@@ -591,9 +597,15 @@
     score_row = score_weight.reshape(1, hid)
     table_t = rel_table.T
     tick = call(tick_kernel, "tick", [(SUBLANES, LANES)], 10**10)
-    outgoing = call(
-        send_kernel, "send", [(nodes, bound, width_all)], 10**9, tick, send_list[0], state_in
-    )
+    hot = call(
+        wanted_kernel,
+        "wanted",
+        [jax.ShapeDtypeStruct((nodes * bound, ent), BF16)],
+        1,
+        tick,
+        send_list[0],
+    )
+    outgoing = call(send_kernel, "send", [(nodes, bound, width_all)], 10**9, hot, state_in)
     received = swap(outgoing, "nodes").reshape(nodes * bound, width_all)
     local, relation, prep, marks = call(
         functools.partial(early_kernel, (chunk,)),

time: 51.7 us -> 51.6 us (level)
    pallas_call x8 -> x9, Pallas kernels: 11.8 us -> 11.9 us  [call(): pl.pallas_call(kernel, out_shape=tuple((dims if isinstance(dims, jax.Shap...]
where the time goes in v5:
time: 51.6 us; the launch traced here: 51.3 us
  blocking collectives  23.8 us (46%)
  Pallas kernels  11.9 us (23%)
  starting transfers between devices  8.48 us (16%)
  waiting for transfers between devices  4.87 us (9%)
  between operations  1.53 us (3%)
  local copies, waits for them, and re-layouts  0.74 us (1%)
    all_to_all x2, blocking collectives, swap(): return lax.all_to_all(values, axes, split_axis=0, concat_axis=0, tiled=True)  23.8 us
    pallas_call x9, Pallas kernels, call(): pl.pallas_call(kernel, out_shape=tuple((dims if isinstance(dims, jax.Shap...  11.9 us
    all_to_all x2, starting transfers between devices, swap(): return lax.all_to_all(values, axes, split_axis=0, concat_axis=0, tiled=True)  8.48 us
    all_to_all x2, waiting for transfers between devices, swap(): return lax.all_to_all(values, axes, split_axis=0, concat_axis=0, tiled=True)  4.87 us
  transfers between devices with their start and end apart: 2, of which 2 were waited for; matrix products, arithmetic and copies ran while one was open for 0% of the time, Pallas kernels for 11%

profile of v5, /device:TPU:0, one launch (start us, length us, event | category | flops | bytes accessed | tf_op | source)
XLA Modules:
  0.0 51.3 jit_solution(11184515303947515926)
XLA Ops:
  0.7 0.7 %copy-done = s32[1,8,64]{2,1,0:T(8,128)S(1)} copy-done((s32[1,8,64]{2,1,0:T(8,128)S(1)}, s32[1,8,64]{2,1,0:T(8,128)}, u32[]{:S(2)}) %copy-start) | copy-done | bytes 2072
  1.3 0.2 wanted.1.hot_ref
  1.6 0.0 copy-start.2
  1.6 0.0 copy-start.3
  1.6 0.0 copy-start.5
  1.6 0.0 copy-start.6
  1.6 0.0 copy-start.7
  1.6 0.0 copy-start.8
  1.6 0.0 copy-start.10
  1.7 0.0 copy-start.11
  1.7 0.0 copy-start.12
  1.7 1.0 %send.1 = f32[8,64,128]{2,1,0:T(8,128)} custom-call(bf16[512,256]{1,0:T(8,128)(2,1)S(1)} %wanted.1.hot_ref, f32[256,128]{1,0:T(8,128)S(1)} %copy-done.1), custom_call_target="tpu_custom_call" | custom-call | flops 1000000000 | bytes 1048576 | tf_op jit(solution)/shard_map/send/pallas_call | solution.py:544
  2.7 5.2 %all-to-all-start = ((f32[8,64,128]{2,1,0:T(8,128)}), f32[8,64,128]{2,1,0:T(8,128)S(1)}, u32[]{:S(2)}, u32[]{:S(2)}) async-start(f32[8,64,128]{2,1,0:T(8,128)} %send.1), calls=%async_computation | async-start | bytes 524288 | tf_op jit(solution)/shard_map/all_to_all | solution.py:562
  8.6 0.0 copy-start.4
  8.6 2.1 %early.1 = (f32[128,4096]{1,0:T(8,128)S(1)}, f32[32,4096]{1,0:T(8,128)S(1)}, f32[160,128]{1,0:T(8,128)S(1)}, s32[8,128]{1,0:T(8,128)S(1)}) custom-call(f32[256,128]{1,0:T(8,128)S(1)} %copy-done.1, s32[1,4096]{1,0:T(1,128)S(1)} %bitcast.19, s32[1,4096]{1,0:T(1,128)S(1)} %bitcast.23, f32[32,535]{1,0:T(8,128)S(1)} %bitcast.18, s32[1,4]{1,0:T(1,128)S(1)} %bitcast.25, ...), custom_call_target="tpu_custom_call" | custom-call | flops 4000000000 | bytes 1048576 | tf_op jit(solution)/shard_map/early/pallas_call | solution.py:544
  10.8 4.1 %all-to-all-done = f32[8,64,128]{2,1,0:T(8,128)S(1)} async-done(((f32[8,64,128]{2,1,0:T(8,128)}), f32[8,64,128]{2,1,0:T(8,128)S(1)}, u32[]{:S(2)}, u32[]{:S(2)}) %all-to-all-start) | async-done | bytes 262176 | tf_op jit(solution)/shard_map/all_to_all | solution.py:562
  14.8 4.0 %forward.1 = (f32[128,4096]{1,0:T(8,128)S(1)}, f32[32,4096]{1,0:T(8,128)S(1)}, bf16[128,256]{1,0:T(8,128)(2,1)S(1)}, f32[16,128]{1,0:T(8,128)S(1)}, f32[8,1,128]{2,1,0:T(1,128)}) custom-call(s32[1,1]{1,0:T(1,128)} %bitcast.14.count_ref, f32[256,128]{1,0:T(8,128)S(1)} %copy-done.1, ...), custom_call_target="tpu_custom_call", output_to_operand_aliasing={{0}: (6, {}), {1}: (7, {})} | custom-call | flops 4000000000 | bytes 1048576 | tf_op jit(solution)/shard_map/forward/pallas_call | solution.py:544
  18.8 3.3 %all-to-all-start.1 = ((f32[8,1,128]{2,1,0:T(1,128)}), f32[8,1,128]{2,1,0:T(1,128)S(1)}, u32[]{:S(2)}, u32[]{:S(2)}) async-start(f32[8,1,128]{2,1,0:T(1,128)} %get-tuple-element.33), calls=%async_computation.1 | async-start | bytes 8192 | tf_op jit(solution)/shard_map/all_to_all | solution.py:562
  22.1 3.7 %backward.1 = (f32[160,896]{1,0:T(8,128)S(1)}, f32[256,128]{1,0:T(8,128)}) custom-call(s32[1,1]{1,0:T(1,128)} %bitcast.15.count_ref, f32[128,4096]{1,0:T(8,128)S(1)} %get-tuple-element.28.srct_ref, s32[1,4096]{1,0:T(1,128)S(1)} %bitcast.22, s32[1,4096]{1,0:T(1,128)S(1)} %bitcast.24, s32[4,128]{1,0:T(4,128)S(1)} %copy-done.9, ...), custom_call_target="tpu_custom_call" | custom-call | flops 4000000000 | bytes 1048576 | tf_op jit(solution)/shard_map/backward/pallas_call | solution.py:544
  25.8 0.8 %all-to-all-done.1.totals_ref = f32[8,1,128]{2,1,0:T(1,128)S(1)} async-done(((f32[8,1,128]{2,1,0:T(1,128)}), f32[8,1,128]{2,1,0:T(1,128)S(1)}, u32[]{:S(2)}, u32[]{:S(2)}) %all-to-all-start.1) | async-done | bytes 4128 | tf_op jit(solution)/shard_map/all_to_all | solution.py:562
  26.6 0.1 combine.1
  26.7 13.7 %all_to_all.20.parts_ref = f32[32,8,128]{2,1,0:T(8,128)S(1)} all-to-all(f32[32,8,128]{2,1,0:T(8,128)S(1)} %combine.1), channel_id=1, replica_groups=mesh['nodes'=8,'queries'=4] {'nodes','queries'}, dimensions={0} | all-to-all | bytes 262144 | tf_op jit(solution)/shard_map/all_to_all | solution.py:562
  40.4 10.1 %all_to_all.21.tiles_ref = f32[32,8,128]{2,1,0:T(8,128)S(1)} all-to-all(f32[32,8,128]{2,1,0:T(8,128)S(1)} %spread.1), channel_id=1, replica_groups=mesh['nodes'=8,'queries'=4] {'nodes','queries'}, dimensions={0} | all-to-all | bytes 262144 | tf_op jit(solution)/shard_map/all_to_all | solution.py:562
  50.5 0.8 %unpack.1 = (f32[32,535]{1,0:T(8,128)}, f32[32,32]{1,0:T(8,128)}, f32[32,64]{1,0:T(8,128)}, f32[32,64]{1,0:T(8,128)}, f32[1,64]{1,0:T(1,128)}, /*index=5*/f32[1,4]{1,0:T(1,128)}) custom-call(f32[32,8,128]{2,1,0:T(8,128)S(1)} %all_to_all.21.tiles_ref, f32[8,1,128]{2,1,0:T(1,128)S(1)} %all-to-all-done.1.totals_ref), custom_call_target="tpu_custom_call" | custom-call | flops 1000000 | bytes 1000000 | tf_op jit(solution)/shard_map/unpack/pallas_call | solution.py:544
  (19 shorter events, 0.1 us)
Async XLA Ops:
  0.6 0.7 %copy-start = (s32[1,8,64]{2,1,0:T(8,128)S(1)}, s32[1,8,64]{2,1,0:T(8,128)}, u32[]{:S(2)}) copy-start(s32[1,8,64]{2,1,0:T(8,128)} %param.20) | copy-start | bytes 6148
  0.6 0.9 %copy-start.1 = (f32[256,128]{1,0:T(8,128)S(1)}, f32[256,128]{1,0:T(8,128)}, u32[]{:S(2)}) copy-start(f32[256,128]{1,0:T(8,128)} %state_ref.5) | copy-start | bytes 393220
  1.6 6.9 %copy-start.2 = (f32[535,32]{0,1:T(8,128)S(1)}, f32[535,32]{0,1:T(8,128)}, u32[]{:S(2)}) copy-start(f32[535,32]{0,1:T(8,128)} %param.25) | copy-start | bytes 205444
  1.6 6.9 %copy-start.3 = (s32[4096]{0:T(1024)S(1)}, s32[4096]{0:T(1024)}, u32[]{:S(2)}) copy-start(s32[4096]{0:T(1024)} %param.16) | copy-start | bytes 49156
  1.6 6.9 %copy-start.5 = (s32[4096]{0:T(1024)S(1)}, s32[4096]{0:T(1024)}, u32[]{:S(2)}) copy-start(s32[4096]{0:T(1024)} %param.18) | copy-start | bytes 49156
  1.6 6.9 %copy-start.6 = (f32[32,32]{1,0:T(8,128)S(1)}, f32[32,32]{1,0:T(8,128)}, u32[]{:S(2)}) copy-start(f32[32,32]{1,0:T(8,128)} %layer_ref.5) | copy-start | bytes 12292
  1.6 6.9 %copy-start.7 = (f32[32,64]{1,0:T(8,128)S(1)}, f32[32,64]{1,0:T(8,128)}, u32[]{:S(2)}) copy-start(f32[32,64]{1,0:T(8,128)} %ment_ref.5) | copy-start | bytes 24580
  1.6 6.9 %copy-start.8 = (f32[32,64]{1,0:T(8,128)S(1)}, f32[32,64]{1,0:T(8,128)}, u32[]{:S(2)}) copy-start(f32[32,64]{1,0:T(8,128)} %mquery_ref.3) | copy-start | bytes 24580
  1.6 6.9 %copy-start.10 = (s32[4]{0:T(128)S(1)}, s32[4]{0:T(128)}, u32[]{:S(2)}) copy-start(s32[4]{0:T(128)} %param.21) | copy-start | bytes 52
  1.7 6.9 %copy-start.11 = (s32[4]{0:T(128)S(1)}, s32[4]{0:T(128)}, u32[]{:S(2)}) copy-start(s32[4]{0:T(128)} %param.22) | copy-start | bytes 52
  1.7 6.9 %copy-start.12 = (s32[4]{0:T(128)S(1)}, s32[4]{0:T(128)}, u32[]{:S(2)}) copy-start(s32[4]{0:T(128)} %param.23) | copy-start | bytes 52
  1.7 6.9 %copy-start.13 = (f32[64]{0:T(128)S(1)}, f32[64]{0:T(128)}, u32[]{:S(2)}) copy-start(f32[64]{0:T(128)} %param.29) | copy-start | bytes 772
  2.7 12.1 %all-to-all-start = ((f32[8,64,128]{2,1,0:T(8,128)}), f32[8,64,128]{2,1,0:T(8,128)S(1)}, u32[]{:S(2)}, u32[]{:S(2)}) async-start(f32[8,64,128]{2,1,0:T(8,128)} %send.1), calls=%async_computation | async-start | bytes 524288 | tf_op jit(solution)/shard_map/all_to_all | solution.py:562
  8.6 6.2 %copy-start.4 = (s32[4096]{0:T(1024)S(1)}, s32[4096]{0:T(1024)}, u32[]{:S(2)}) copy-start(s32[4096]{0:T(1024)} %param.17) | copy-start | bytes 49156
  8.6 6.2 %copy-start.9 = (s32[4,128]{1,0:T(4,128)S(1)}, s32[4,128]{1,0:T(4,128)}, u32[]{:S(2)}) copy-start(s32[4,128]{1,0:T(4,128)} %neg_ref.3) | copy-start | bytes 6148
  18.8 7.8 %all-to-all-start.1 = ((f32[8,1,128]{2,1,0:T(1,128)}), f32[8,1,128]{2,1,0:T(1,128)S(1)}, u32[]{:S(2)}, u32[]{:S(2)}) async-start(f32[8,1,128]{2,1,0:T(1,128)} %get-tuple-element.33), calls=%async_computation.1 | async-start | bytes 8192 | tf_op jit(solution)/shard_map/all_to_all | solution.py:562

commit v6 on v5

--- a/solution.py
+++ b/solution.py
@@ -692,7 +692,7 @@
         all_totals,
         grads,
     )
-    axes = ("nodes", "queries") if group == wide else "nodes"
+    axes = ("queries", "nodes") if group == wide else "nodes"
     own = held // group
     parts = swap(sent, axes).reshape(group, own * SUBLANES, LANES)
     if group == wide:

time: 51.6 us -> 51.4 us (level)
  no operation moved by 1% of the time
where the time goes in v6:
time: 51.4 us; the launch traced here: 51 us
  blocking collectives  23.5 us (46%)
  Pallas kernels  11.9 us (23%)
  starting transfers between devices  8.48 us (16%)
  waiting for transfers between devices  4.87 us (9%)
  between operations  1.53 us (3%)
  local copies, waits for them, and re-layouts  0.74 us (1%)
    all_to_all x2, blocking collectives, swap(): return lax.all_to_all(values, axes, split_axis=0, concat_axis=0, tiled=True)  23.5 us
    pallas_call x9, Pallas kernels, call(): pl.pallas_call(kernel, out_shape=tuple((dims if isinstance(dims, jax.Shap...  11.9 us
    all_to_all x2, starting transfers between devices, swap(): return lax.all_to_all(values, axes, split_axis=0, concat_axis=0, tiled=True)  8.48 us
    all_to_all x2, waiting for transfers between devices, swap(): return lax.all_to_all(values, axes, split_axis=0, concat_axis=0, tiled=True)  4.87 us
  transfers between devices with their start and end apart: 2, of which 2 were waited for; matrix products, arithmetic and copies ran while one was open for 0% of the time, Pallas kernels for 11%

profile of v6, /device:TPU:0, one launch (start us, length us, event | category | flops | bytes accessed | tf_op | source)
XLA Modules:
  0.0 51.0 jit_solution(1019501233162690463)
XLA Ops:
  0.7 0.7 %copy-done = s32[1,8,64]{2,1,0:T(8,128)S(1)} copy-done((s32[1,8,64]{2,1,0:T(8,128)S(1)}, s32[1,8,64]{2,1,0:T(8,128)}, u32[]{:S(2)}) %copy-start) | copy-done | bytes 2072
  1.3 0.2 wanted.1.hot_ref
  1.6 0.0 copy-start.2
  1.6 0.0 copy-start.3
  1.6 0.0 copy-start.5
  1.6 0.0 copy-start.6
  1.6 0.0 copy-start.7
  1.6 0.0 copy-start.8
  1.6 0.0 copy-start.10
  1.7 0.0 copy-start.11
  1.7 0.0 copy-start.12
  1.7 1.0 %send.1 = f32[8,64,128]{2,1,0:T(8,128)} custom-call(bf16[512,256]{1,0:T(8,128)(2,1)S(1)} %wanted.1.hot_ref, f32[256,128]{1,0:T(8,128)S(1)} %copy-done.1), custom_call_target="tpu_custom_call" | custom-call | flops 1000000000 | bytes 1048576 | tf_op jit(solution)/shard_map/send/pallas_call | solution.py:544
  2.7 5.2 %all-to-all-start = ((f32[8,64,128]{2,1,0:T(8,128)}), f32[8,64,128]{2,1,0:T(8,128)S(1)}, u32[]{:S(2)}, u32[]{:S(2)}) async-start(f32[8,64,128]{2,1,0:T(8,128)} %send.1), calls=%async_computation | async-start | bytes 524288 | tf_op jit(solution)/shard_map/all_to_all | solution.py:562
  8.6 0.0 copy-start.4
  8.6 2.1 %early.1 = (f32[128,4096]{1,0:T(8,128)S(1)}, f32[32,4096]{1,0:T(8,128)S(1)}, f32[160,128]{1,0:T(8,128)S(1)}, s32[8,128]{1,0:T(8,128)S(1)}) custom-call(f32[256,128]{1,0:T(8,128)S(1)} %copy-done.1, s32[1,4096]{1,0:T(1,128)S(1)} %bitcast.19, s32[1,4096]{1,0:T(1,128)S(1)} %bitcast.23, f32[32,535]{1,0:T(8,128)S(1)} %bitcast.18, s32[1,4]{1,0:T(1,128)S(1)} %bitcast.25, ...), custom_call_target="tpu_custom_call" | custom-call | flops 4000000000 | bytes 1048576 | tf_op jit(solution)/shard_map/early/pallas_call | solution.py:544
  10.8 4.1 %all-to-all-done = f32[8,64,128]{2,1,0:T(8,128)S(1)} async-done(((f32[8,64,128]{2,1,0:T(8,128)}), f32[8,64,128]{2,1,0:T(8,128)S(1)}, u32[]{:S(2)}, u32[]{:S(2)}) %all-to-all-start) | async-done | bytes 262176 | tf_op jit(solution)/shard_map/all_to_all | solution.py:562
  14.8 4.0 %forward.1 = (f32[128,4096]{1,0:T(8,128)S(1)}, f32[32,4096]{1,0:T(8,128)S(1)}, bf16[128,256]{1,0:T(8,128)(2,1)S(1)}, f32[16,128]{1,0:T(8,128)S(1)}, f32[8,1,128]{2,1,0:T(1,128)}) custom-call(s32[1,1]{1,0:T(1,128)} %bitcast.14.count_ref, f32[256,128]{1,0:T(8,128)S(1)} %copy-done.1, ...), custom_call_target="tpu_custom_call", output_to_operand_aliasing={{0}: (6, {}), {1}: (7, {})} | custom-call | flops 4000000000 | bytes 1048576 | tf_op jit(solution)/shard_map/forward/pallas_call | solution.py:544
  18.8 3.3 %all-to-all-start.1 = ((f32[8,1,128]{2,1,0:T(1,128)}), f32[8,1,128]{2,1,0:T(1,128)S(1)}, u32[]{:S(2)}, u32[]{:S(2)}) async-start(f32[8,1,128]{2,1,0:T(1,128)} %get-tuple-element.33), calls=%async_computation.1 | async-start | bytes 8192 | tf_op jit(solution)/shard_map/all_to_all | solution.py:562
  22.1 3.7 %backward.1 = (f32[160,896]{1,0:T(8,128)S(1)}, f32[256,128]{1,0:T(8,128)}) custom-call(s32[1,1]{1,0:T(1,128)} %bitcast.15.count_ref, f32[128,4096]{1,0:T(8,128)S(1)} %get-tuple-element.28.srct_ref, s32[1,4096]{1,0:T(1,128)S(1)} %bitcast.22, s32[1,4096]{1,0:T(1,128)S(1)} %bitcast.24, s32[4,128]{1,0:T(4,128)S(1)} %copy-done.9, ...), custom_call_target="tpu_custom_call" | custom-call | flops 4000000000 | bytes 1048576 | tf_op jit(solution)/shard_map/backward/pallas_call | solution.py:544
  25.8 0.8 %all-to-all-done.1.totals_ref = f32[8,1,128]{2,1,0:T(1,128)S(1)} async-done(((f32[8,1,128]{2,1,0:T(1,128)}), f32[8,1,128]{2,1,0:T(1,128)S(1)}, u32[]{:S(2)}, u32[]{:S(2)}) %all-to-all-start.1) | async-done | bytes 4128 | tf_op jit(solution)/shard_map/all_to_all | solution.py:562
  26.6 0.1 combine.1
  26.7 13.5 %all_to_all.20.parts_ref = f32[32,8,128]{2,1,0:T(8,128)S(1)} all-to-all(f32[32,8,128]{2,1,0:T(8,128)S(1)} %combine.1), channel_id=1, replica_groups=mesh['nodes'=8,'queries'=4] {'queries','nodes'}, dimensions={0} | all-to-all | bytes 262144 | tf_op jit(solution)/shard_map/all_to_all | solution.py:562
  40.3 10.0 %all_to_all.21.tiles_ref = f32[32,8,128]{2,1,0:T(8,128)S(1)} all-to-all(f32[32,8,128]{2,1,0:T(8,128)S(1)} %spread.1), channel_id=1, replica_groups=mesh['nodes'=8,'queries'=4] {'queries','nodes'}, dimensions={0} | all-to-all | bytes 262144 | tf_op jit(solution)/shard_map/all_to_all | solution.py:562
  50.3 0.8 %unpack.1 = (f32[32,535]{1,0:T(8,128)}, f32[32,32]{1,0:T(8,128)}, f32[32,64]{1,0:T(8,128)}, f32[32,64]{1,0:T(8,128)}, f32[1,64]{1,0:T(1,128)}, /*index=5*/f32[1,4]{1,0:T(1,128)}) custom-call(f32[32,8,128]{2,1,0:T(8,128)S(1)} %all_to_all.21.tiles_ref, f32[8,1,128]{2,1,0:T(1,128)S(1)} %all-to-all-done.1.totals_ref), custom_call_target="tpu_custom_call" | custom-call | flops 1000000 | bytes 1000000 | tf_op jit(solution)/shard_map/unpack/pallas_call | solution.py:544
  (19 shorter events, 0.1 us)
Async XLA Ops:
  0.6 0.7 %copy-start = (s32[1,8,64]{2,1,0:T(8,128)S(1)}, s32[1,8,64]{2,1,0:T(8,128)}, u32[]{:S(2)}) copy-start(s32[1,8,64]{2,1,0:T(8,128)} %param.20) | copy-start | bytes 6148
  0.6 0.9 %copy-start.1 = (f32[256,128]{1,0:T(8,128)S(1)}, f32[256,128]{1,0:T(8,128)}, u32[]{:S(2)}) copy-start(f32[256,128]{1,0:T(8,128)} %state_ref.5) | copy-start | bytes 393220
  1.6 6.9 %copy-start.2 = (f32[535,32]{0,1:T(8,128)S(1)}, f32[535,32]{0,1:T(8,128)}, u32[]{:S(2)}) copy-start(f32[535,32]{0,1:T(8,128)} %param.25) | copy-start | bytes 205444
  1.6 6.9 %copy-start.3 = (s32[4096]{0:T(1024)S(1)}, s32[4096]{0:T(1024)}, u32[]{:S(2)}) copy-start(s32[4096]{0:T(1024)} %param.16) | copy-start | bytes 49156
  1.6 6.9 %copy-start.5 = (s32[4096]{0:T(1024)S(1)}, s32[4096]{0:T(1024)}, u32[]{:S(2)}) copy-start(s32[4096]{0:T(1024)} %param.18) | copy-start | bytes 49156
  1.6 6.9 %copy-start.6 = (f32[32,32]{1,0:T(8,128)S(1)}, f32[32,32]{1,0:T(8,128)}, u32[]{:S(2)}) copy-start(f32[32,32]{1,0:T(8,128)} %layer_ref.5) | copy-start | bytes 12292
  1.6 6.9 %copy-start.7 = (f32[32,64]{1,0:T(8,128)S(1)}, f32[32,64]{1,0:T(8,128)}, u32[]{:S(2)}) copy-start(f32[32,64]{1,0:T(8,128)} %ment_ref.5) | copy-start | bytes 24580
  1.6 6.9 %copy-start.8 = (f32[32,64]{1,0:T(8,128)S(1)}, f32[32,64]{1,0:T(8,128)}, u32[]{:S(2)}) copy-start(f32[32,64]{1,0:T(8,128)} %mquery_ref.3) | copy-start | bytes 24580
  1.6 6.9 %copy-start.10 = (s32[4]{0:T(128)S(1)}, s32[4]{0:T(128)}, u32[]{:S(2)}) copy-start(s32[4]{0:T(128)} %param.21) | copy-start | bytes 52
  1.7 6.9 %copy-start.11 = (s32[4]{0:T(128)S(1)}, s32[4]{0:T(128)}, u32[]{:S(2)}) copy-start(s32[4]{0:T(128)} %param.22) | copy-start | bytes 52
  1.7 6.9 %copy-start.12 = (s32[4]{0:T(128)S(1)}, s32[4]{0:T(128)}, u32[]{:S(2)}) copy-start(s32[4]{0:T(128)} %param.23) | copy-start | bytes 52
  1.7 6.9 %copy-start.13 = (f32[64]{0:T(128)S(1)}, f32[64]{0:T(128)}, u32[]{:S(2)}) copy-start(f32[64]{0:T(128)} %param.29) | copy-start | bytes 772
  2.7 12.1 %all-to-all-start = ((f32[8,64,128]{2,1,0:T(8,128)}), f32[8,64,128]{2,1,0:T(8,128)S(1)}, u32[]{:S(2)}, u32[]{:S(2)}) async-start(f32[8,64,128]{2,1,0:T(8,128)} %send.1), calls=%async_computation | async-start | bytes 524288 | tf_op jit(solution)/shard_map/all_to_all | solution.py:562
  8.6 6.2 %copy-start.4 = (s32[4096]{0:T(1024)S(1)}, s32[4096]{0:T(1024)}, u32[]{:S(2)}) copy-start(s32[4096]{0:T(1024)} %param.17) | copy-start | bytes 49156
  8.6 6.2 %copy-start.9 = (s32[4,128]{1,0:T(4,128)S(1)}, s32[4,128]{1,0:T(4,128)}, u32[]{:S(2)}) copy-start(s32[4,128]{1,0:T(4,128)} %neg_ref.3) | copy-start | bytes 6148
  18.8 7.8 %all-to-all-start.1 = ((f32[8,1,128]{2,1,0:T(1,128)}), f32[8,1,128]{2,1,0:T(1,128)S(1)}, u32[]{:S(2)}, u32[]{:S(2)}) async-start(f32[8,1,128]{2,1,0:T(1,128)} %get-tuple-element.33), calls=%async_computation.1 | async-start | bytes 8192 | tf_op jit(solution)/shard_map/all_to_all | solution.py:562
